TPU v7x, 128 devices: a whole 4x4x4 slice. The times are simulated.
128 devices in a mesh: row: 8 (over z, core), col: 16 (over x, y).
Axes of the slice: x: 4, y: 4, z: 4, core: 2. Of those that a mesh axis runs over, the one named last changes fastest.
Arguments:
- object_tiles: float32 [3, 2, 1024, 2048], P(None, None, 'row', 'col'), may hold values from -1 to 1
- probe_wave: float32 [2, 256, 256], replicated, may hold values from -6 to 6
- slot_counts: int32 [8, 16], P('row', 'col'), may hold values from 0 to 2, as said below
- slot_offsets: int32 [8, 16, 2, 2], P('row', 'col'), may hold values from 0 to 1792, as said below
- amplitudes: float32 [8, 16, 2, 256, 256], P('row', 'col'), may hold values from 0 to 2
Outputs:
- object_grad: float32 [3, 2, 1024, 2048], P(None, None, 'row', 'col')
- probe_grad: float32 [2, 256, 256], replicated
Inputs may be any that keep to these rules, and one draw needn't show every extreme that they name: `slot_counts`: the live slots of a tile are its first slots; the two tiles at columns 2j and 2j+1 of the same tile row hold 2 positions together. `slot_offsets`: every slot of tile (r, c), live or not, holds a corner whose 256 x 256 patch lies inside the object and inside the tile's rows r * 128 .. (r + 1) * 128 - 1 and columns c * 128 .. (c + 1) * 128 - 1 widened by 128 cells on every side.
All inputs are finite; a program needn't handle non-finite values.
Results may differ from a plain program's by a relative error of at most 0.0003.
Values sent between devices are 32-bit elements; how exact they have to be, the bound alone decides.
A program may use at most 64 MiB of HBM per device.

v0:
```python
import math

import jax
import jax.numpy as jnp
from jax import lax
from jax.sharding import PartitionSpec as P

FLOOR = 0.2
HIGHEST = lax.Precision.HIGHEST


def padded_2(block, sides, width):
    for axis, dim in sides:
        count = lax.axis_size(axis)
        forward = [(i, i + 1) for i in range(count - 1)]
        backward = [(target, source) for source, target in forward]
        low = lax.ppermute(
            lax.slice_in_dim(block, block.shape[dim] - width, None, axis=dim), axis, forward
        )
        high = lax.ppermute(lax.slice_in_dim(block, 0, width, axis=dim), axis, backward)
        block = jnp.concatenate([low, block, high], axis=dim)
    return block


def phase_table(length):
    index = jnp.arange(length, dtype=jnp.int32)
    signed = jnp.where(index < length // 2, index, index - length)
    return (signed * signed).astype(jnp.float32) * (math.pi / (2.0 * length))


def turn_angles(length):
    index = jnp.arange(length, dtype=jnp.int32)
    turns = index[:, None] * index[None, :] % length
    return turns.astype(jnp.float32) * (2.0 * math.pi / length)


def fourier_matrix(length):
    angle = turn_angles(length)
    factor = 1.0 / math.sqrt(length)
    return (jnp.cos(angle) * factor, -jnp.sin(angle) * factor)


def fresnel_matrix(length):
    angle = turn_angles(length)
    phase = phase_table(length)
    cos_phase, sin_phase = (jnp.cos(phase), jnp.sin(phase))
    cos_turn, sin_turn = (jnp.cos(angle), jnp.sin(angle))
    real_lag = (
        jnp.dot(cos_phase, cos_turn, precision=HIGHEST)
        + jnp.dot(sin_phase, sin_turn, precision=HIGHEST)
    ) / length
    imag_lag = (
        jnp.dot(cos_phase, sin_turn, precision=HIGHEST)
        - jnp.dot(sin_phase, cos_turn, precision=HIGHEST)
    ) / length
    index = jnp.arange(length, dtype=jnp.int32)
    lag_index = (index[:, None] - index[None, :]) % length
    return (real_lag[lag_index], imag_lag[lag_index])


def multiply_left(left, right):
    return jnp.einsum("jk,bkl->bjl", left, right, precision=HIGHEST)


def multiply_right(left, right):
    return jnp.einsum("bjk,kl->bjl", left, right, precision=HIGHEST)


def sandwich(matrix, wave):
    real_m, imag_m = matrix
    real_w, imag_w = (wave[:, 0], wave[:, 1])
    real_a = multiply_left(real_m, real_w) - multiply_left(imag_m, imag_w)
    imag_a = multiply_left(real_m, imag_w) + multiply_left(imag_m, real_w)
    real_b = multiply_right(real_a, real_m) - multiply_right(imag_a, imag_m)
    imag_b = multiply_right(real_a, imag_m) + multiply_right(imag_a, real_m)
    return jnp.stack([real_b, imag_b], axis=1)


def adjoint(matrix):
    return (matrix[0], -matrix[1])


def complex_times(first, second):
    return jnp.stack(
        [
            first[:, 0] * second[:, 0] - first[:, 1] * second[:, 1],
            first[:, 0] * second[:, 1] + first[:, 1] * second[:, 0],
        ],
        axis=1,
    )


def conj_times(first, second):
    return jnp.stack(
        [
            first[:, 0] * second[:, 0] + first[:, 1] * second[:, 1],
            first[:, 0] * second[:, 1] - first[:, 1] * second[:, 0],
        ],
        axis=1,
    )


def patch_gradients(work, work_amps, weight, probe_wave):
    length = probe_wave.shape[-1]
    layers = work.shape[1]
    fresnel = fresnel_matrix(length)
    fourier = fourier_matrix(length)
    front = probe_wave[None]
    inputs = []
    wave = front
    for layer in range(layers):
        if layer > 0:
            wave = sandwich(fresnel, wave)
        inputs.append(wave)
        wave = complex_times(wave, work[:, layer])
    far = sandwich(fourier, wave)
    modulus = jnp.sqrt(far[:, 0] * far[:, 0] + far[:, 1] * far[:, 1])
    factor = (1.0 - work_amps / jnp.maximum(modulus, FLOOR)) * weight[:, None, None]
    back = sandwich(adjoint(fourier), far * factor[:, None])
    grads = [None] * layers
    for layer in reversed(range(layers)):
        grads[layer] = conj_times(inputs[layer], back)
        back = conj_times(work[:, layer], back)
        if layer > 0:
            back = sandwich(adjoint(fresnel), back)
    return (jnp.stack(grads, axis=1), jnp.sum(back, axis=0))


def on_device(object_tiles, probe_wave, slot_counts, slot_offsets, amplitudes):
    layers, pairs, tile_rows, tile_cols = object_tiles.shape
    length = probe_wave.shape[-1]
    margin = length // 2
    capacity = slot_offsets.shape[2]
    count = slot_counts[0, 0]
    corners = slot_offsets[0, 0]
    measured = amplitudes[0, 0]
    base_row = lax.axis_index("row") * tile_rows - margin
    base_col = lax.axis_index("col") * tile_cols - margin
    local_rows = corners[:, 0] - base_row
    local_cols = corners[:, 1] - base_col
    zero = jnp.zeros((), jnp.int32)
    window = (layers, pairs, length, length)
    extended = padded_2(object_tiles, (("row", 2), ("col", 3)), margin)
    patches = jnp.stack(
        [
            lax.dynamic_slice(extended, (zero, zero, local_rows[which], local_cols[which]), window)
            for which in range(capacity)
        ]
    )
    weight = (jnp.arange(capacity, dtype=jnp.int32) < count).astype(jnp.float32)
    grad_slots, probe_local = patch_gradients(patches, measured, weight, probe_wave)
    grad_ext = jnp.zeros_like(extended)
    for which in range(capacity):
        start = (zero, zero, local_rows[which], local_cols[which])
        piece = lax.dynamic_slice(grad_ext, start, window) + grad_slots[which]
        grad_ext = lax.dynamic_update_slice(grad_ext, piece, start)
    padded = padded_2(grad_ext, (("row", 2), ("col", 3)), margin)
    double = 2 * margin
    middle = padded[:, :, double : double + tile_rows, :]
    middle = middle.at[:, :, :margin, :].add(padded[:, :, :margin, :])
    middle = middle.at[:, :, tile_rows - margin :, :].add(padded[:, :, tile_rows + 3 * margin :, :])
    result = middle[:, :, :, double : double + tile_cols]
    result = result.at[:, :, :, :margin].add(middle[:, :, :, :margin])
    result = result.at[:, :, :, tile_cols - margin :].add(middle[:, :, :, tile_cols + 3 * margin :])
    probe_total = lax.psum(probe_local, ("row", "col"))
    return (result, probe_total)


def solution(mesh):
    return jax.shard_map(
        on_device,
        mesh=mesh,
        in_specs=(
            P(None, None, "row", "col"),
            P(),
            P("row", "col"),
            P("row", "col", None, None),
            P("row", "col", None, None, None),
        ),
        out_specs=(P(None, None, "row", "col"), P()),
        check_vma=False,
    )
```

profile of v0, /device:TPU:1, one launch (start us, length us, event | category | flops | bytes accessed | tf_op | source)
XLA Modules:
  0.0 1169.4 jit_solution(18283133271916978640)
XLA Ops:
  7.2 4.9 collective-permute-start
  12.2 1.9 collective-permute-start.1
  26.9 5.0 collective-permute-start.2
  31.9 406.1 %gather_fusion.1 = f32[65536]{0:T(1024)S(1)} fusion(f32[256]{0:T(256)S(1)} %subtract_multiply_fusion, s32[65536]{0:T(1024)S(1)} %broadcast_clamp_fusion), kind=kCustom, calls=%fused_computation.1 | custom fusion | bytes 786432 | tf_op jit(solution)/shard_map/gather | solution.py:58
  441.3 406.6 %gather_fusion = f32[65536]{0:T(1024)S(1)} fusion(f32[256]{0:T(256)S(1)} %add_multiply_fusion, s32[65536]{0:T(1024)S(1)} %broadcast_clamp_fusion), kind=kCustom, calls=%fused_computation | custom fusion | bytes 786432 | tf_op jit(solution)/shard_map/gather | solution.py:58
  850.5 2.2 pad_maximum_fusion
  876.2 2.1 fusion.45
  883.8 2.0 fusion.19
  887.7 2.2 fusion.20
  899.2 2.1 multiply_subtract_fusion.1
  917.5 2.2 add_bitcast_fusion
  922.4 19.7 %dynamic_update_slice.6 = f32[3,2,384,384]{3,2,1,0:T(8,128)S(1)} dynamic-update-slice(f32[3,2,384,384]{3,2,1,0:T(8,128)S(1)} %broadcast_in_dim.4, f32[3,2,256,256]{3,2,1,0:T(8,128)} %slice_bitcast_fusion.1, s32[]{:T(128)} %constant.175.clone.1, s32[]{:T(128)} %constant.175.clone.1, s32[]{:T(128)S(6)} %select_n.101, s32[]{:T(128)S(6)} %select_n.102) | dynamic-update-slice | bytes 3145732 | tf_op jit(solution)/shard_map/dynamic_update_slice | solution.py:156
  942.1 3.1 fusion
  945.2 17.6 %dynamic_update_slice.7 = f32[3,2,384,384]{3,2,1,0:T(8,128)S(1)} dynamic-update-slice(f32[3,2,384,384]{3,2,1,0:T(8,128)S(1)} %dynamic_update_slice.6, f32[3,2,256,256]{3,2,1,0:T(8,128)} %fusion, s32[]{:T(128)} %constant.175.clone.1, s32[]{:T(128)} %constant.175.clone.1, s32[]{:T(128)S(6)} %select_n.103, s32[]{:T(128)S(6)} %select_n.104) | dynamic-update-slice | bytes 3145732 | tf_op jit(solution)/shard_map/dynamic_update_slice | solution.py:156
  963.0 1.9 collective-permute-start.4
  964.9 2.6 collective-permute-start.5
  967.5 10.5 collective-permute-done.4
  978.0 6.1 collective-permute-done.5
  984.1 2.2 pad_maximum_fusion.4
  986.4 8.9 collective-permute-start.6
  997.5 27.4 %collective-permute-done.6 = f32[3,2,640,128]{3,2,1,0:T(8,128)} collective-permute-done((f32[3,2,640,128]{3,2,1,0:T(8,128)}, f32[3,2,640,128]{3,2,1,0:T(8,128)}, u32[]{:S(2)}, u32[]{:S(2)}) %collective-permute-start.6) | collective-permute-done | bytes 1966112 | tf_op jit(solution)/shard_map/ppermute | solution.py:17
  1024.9 5.8 collective-permute-done.7
  1030.7 2.8 fusion.23
  1033.5 126.9 %all-reduce.2.cloned.1.call-done = f32[2,256,256]{2,1,0:T(8,128)} async-done(((f32[2,256,256]{2,1,0:T(8,128)}), f32[2,256,256]{2,1,0:T(8,128)}) %all-reduce.2.cloned.1.call-update) | async-done | bytes 524304 | tf_op jit(solution)/shard_map/psum | solution.py:165
  (100 shorter events, 73.5 us)
Async XLA Ops:
  7.2 1153.3 %all-reduce.2.cloned.1.call-start = ((), (), s32[]{:S(2)}) async-start(), calls=%async_computation | async-start | bytes 1048576 | tf_op jit(solution)/shard_map/psum | solution.py:165
  7.2 16.0 %collective-permute-start = (f32[3,2,128,128]{3,2,1,0:T(8,128)}, f32[3,2,128,128]{3,2,1,0:T(8,128)S(1)}, u32[]{:S(2)}, u32[]{:S(2)}) collective-permute-start(f32[3,2,128,128]{3,2,1,0:T(8,128)} %param.21), channel_id=1, source_target_pairs={{0,16},{16,32},{32,48},{48,64},{64,80},{80,96},{96,112},{1,17},{17... | collective-permute-start | bytes 1179656 | tf_op jit(solution)/shard_map/ppermute | solution.py:17
  12.2 12.7 %collective-permute-start.1 = (f32[3,2,128,128]{3,2,1,0:T(8,128)}, f32[3,2,128,128]{3,2,1,0:T(8,128)S(1)}, u32[]{:S(2)}, u32[]{:S(2)}) collective-permute-start(f32[3,2,128,128]{3,2,1,0:T(8,128)} %param.21), channel_id=1, source_target_pairs={{16,0},{32,16},{48,32},{64,48},{80,64},{96,80},{112,96},{17,1},{33... | collective-permute-start | bytes 1179656 | tf_op jit(solution)/shard_map/ppermute | solution.py:20
  20.6 3.4 copy-start.6
  25.6 824.8 %collective-permute-start.3 = (f32[3,2,384,128]{3,2,1,0:T(8,128)}, f32[3,2,384,128]{3,2,1,0:T(8,128)}, u32[]{:S(2)}, u32[]{:S(2)}) collective-permute-start(f32[3,2,384,128]{3,2,1,0:T(8,128)} %constant_dynamic-update-slice_fusion), channel_id=1, source_target_pairs={{1,0},{2,1},{3,2},{4,3},{5,4},{6,5},{7,6},{8,7},{9,8},{10,9},{11,1... | collective-permute-start | bytes 3538952 | tf_op jit(solution)/shard_map/ppermute | solution.py:20
  26.9 823.5 %collective-permute-start.2 = (f32[3,2,384,128]{3,2,1,0:T(8,128)}, f32[3,2,384,128]{3,2,1,0:T(8,128)}, u32[]{:S(2)}, u32[]{:S(2)}) collective-permute-start(f32[3,2,384,128]{3,2,1,0:T(8,128)} %constant_dynamic-update-slice_fusion), channel_id=1, source_target_pairs={{0,1},{1,2},{2,3},{3,4},{4,5},{5,6},{6,7},{7,8},{8,9},{9,10},{10,1... | collective-permute-start | bytes 3538952 | tf_op jit(solution)/shard_map/ppermute | solution.py:17
  441.2 409.1 %copy-start.5 = (f32[2,256,256]{2,1,0:T(8,128)S(1)}, f32[2,256,256]{2,1,0:T(8,128)}, u32[]{:S(2)}) copy-start(f32[2,256,256]{2,1,0:T(8,128)} %param.22) | copy-start | bytes 1572868
  878.2 5.6 copy-start.7
  920.0 2.1 copy-start
  963.0 15.1 %collective-permute-start.4 = (f32[3,2,128,384]{3,2,1,0:T(8,128)S(1)}, f32[3,2,128,384]{3,2,1,0:T(8,128)S(1)}, u32[]{:S(2)}, u32[]{:S(2)}) collective-permute-start(f32[3,2,128,384]{3,2,1,0:T(8,128)S(1)} %get-tuple-element.84), channel_id=1, source_target_pairs={{0,16},{16,32},{32,48},{48,64},{64,80},{80,96},{96,112},{1,17},{17... | collective-permute-start | bytes 3538952 | tf_op jit(solution)/shard_map/ppermute | solution.py:17
  964.9 31.7 %copy-start.3 = (f32[2,1,256,256]{3,2,0,1:T(8,128)S(1)}, f32[2,1,256,256]{3,2,0,1:T(8,128)}, u32[]{:S(2)}) copy-start(f32[2,1,256,256]{3,2,0,1:T(8,128)} %get-tuple-element.91) | copy-start | bytes 1572868
  964.9 31.7 %copy-start.4 = (f32[2,1,256,256]{3,2,0,1:T(8,128)S(1)}, f32[2,1,256,256]{3,2,0,1:T(8,128)}, u32[]{:S(2)}) copy-start(f32[2,1,256,256]{3,2,0,1:T(8,128)} %get-tuple-element.92) | copy-start | bytes 1572868
  964.9 19.2 %collective-permute-start.5 = (f32[3,2,128,384]{3,2,1,0:T(8,128)S(1)}, f32[3,2,128,384]{3,2,1,0:T(8,128)S(1)}, u32[]{:S(2)}, u32[]{:S(2)}) collective-permute-start(f32[3,2,128,384]{3,2,1,0:T(8,128)S(1)} %get-tuple-element.85), channel_id=1, source_target_pairs={{16,0},{32,16},{48,32},{64,48},{80,64},{96,80},{112,96},{17,1},{33... | collective-permute-start | bytes 3538952 | tf_op jit(solution)/shard_map/ppermute | solution.py:20
  978.0 6.1 copy-start.1
  984.1 2.2 copy-start.2
  986.4 38.5 %collective-permute-start.6 = (f32[3,2,640,128]{3,2,1,0:T(8,128)}, f32[3,2,640,128]{3,2,1,0:T(8,128)}, u32[]{:S(2)}, u32[]{:S(2)}) collective-permute-start(f32[3,2,640,128]{3,2,1,0:T(8,128)} %get-tuple-element.82), channel_id=1, source_target_pairs={{0,1},{1,2},{2,3},{3,4},{4,5},{5,6},{6,7},{7,8},{8,9},{9,10},{10,1... | collective-permute-start | bytes 5898248 | tf_op jit(solution)/shard_map/ppermute | solution.py:17
  995.3 35.4 %collective-permute-start.7 = (f32[3,2,640,128]{3,2,1,0:T(8,128)}, f32[3,2,640,128]{3,2,1,0:T(8,128)}, u32[]{:S(2)}, u32[]{:S(2)}) collective-permute-start(f32[3,2,640,128]{3,2,1,0:T(8,128)} %get-tuple-element.83), channel_id=1, source_target_pairs={{1,0},{2,1},{3,2},{4,3},{5,4},{6,5},{7,6},{8,7},{9,8},{10,9},{11,1... | collective-permute-start | bytes 5898248 | tf_op jit(solution)/shard_map/ppermute | solution.py:20
Sparse Core Ops, SparseCore 0:
  997.6 162.8 all-reduce.1
where the time goes:
time: 1180 us; the launch traced here: 1170 us
  local copies, waits for them, and re-layouts  859 us (73%)
  waiting for transfers between devices  177 us (15%)
  matrix products  69.8 us (6%)
  starting transfers between devices  27.9 us (2%)
  between operations  23 us (2%)
  other arithmetic  13.3 us (1%)
    gather x5, local copies, waits for them, and re-layouts, fresnel_matrix(): return (real_lag[lag_index], imag_lag[lag_index])  813 us
    psum x1, waiting for transfers between devices, on_device(): probe_total = lax.psum(probe_local, ('row', 'col'))  127 us
    ppermute x4, waiting for transfers between devices, padded_2(): lax.ppermute(lax.slice_in_dim(block, block.shape[dim] - width, None, axis...  37.9 us
    dynamic_update_slice x2, local copies, waits for them, and re-layouts, on_device(): grad_ext = lax.dynamic_update_slice(grad_ext, piece, start)  37.3 us
    dot_general x24, matrix products, multiply_right(): return jnp.einsum('bjk,kl->bjl', left, right, precision=HIGHEST)  33.4 us
    dot_general x24, matrix products, multiply_left(): return jnp.einsum('jk,bkl->bjl', left, right, precision=HIGHEST)  31.7 us
  transfers between devices with their start and end apart: 9, of which 5 were waited for; matrix products, arithmetic and copies ran while one was open for 71% of the time, Pallas kernels for 0%

commit v1 on v0

v1 whole, which is shorter than its diff:
```python
import math

import jax
import jax.numpy as jnp
import ml_dtypes
import numpy as np
from jax import lax
from jax.experimental import pallas as pl
from jax.experimental.pallas import tpu as pltpu
from jax.sharding import PartitionSpec as P

FLOOR = 0.2
N = 256
H = N // 2
SLICES = 3
CAP = 2
MESH = pl.DeviceIdType.MESH
F32 = jnp.float32
BF16 = jnp.bfloat16

FS_R, FD_R, FS_L, FD_L, E_R, O_R, E_L, O_L, OT_R, OT_L = range(10)


def right_form(a):
    return np.block([[a.real, a.imag], [-a.imag, a.real]])


def left_form(a):
    return np.block([[a.real, -a.imag], [a.imag, a.real]])


def constant_matrices():
    index = np.arange(N)
    signed = np.where(index < H, index, index - N).astype(np.float64)
    transfer = np.exp(-1j * math.pi * signed * signed / (2.0 * N))
    lag = np.fft.ifft(transfer)
    circulant = lag[(index[:, None] - index[None, :]) % N]
    sums = (circulant[:H, :H] + circulant[:H, H:]) / 2.0
    diffs = (circulant[:H, :H] - circulant[:H, H:]) / 2.0
    j = np.arange(H)
    turn = np.exp(-2j * math.pi * (j[:, None] * j[None, :] % H) / H) / math.sqrt(N)
    twiddle = np.exp(-2j * math.pi * j / N)
    odd = twiddle[:, None] * turn
    mats = [
        right_form(sums), right_form(diffs), left_form(sums), left_form(diffs),
        right_form(turn), right_form(odd), left_form(turn), left_form(odd.T),
        right_form(odd.T), left_form(odd),
    ]
    full = np.stack(mats).astype(np.float32)
    high = full.astype(ml_dtypes.bfloat16)
    low = (full - high.astype(np.float32)).astype(ml_dtypes.bfloat16)
    order = np.zeros((N, N), np.float32)
    order[2 * j, j] = 1.0
    order[2 * j + 1, H + j] = 1.0
    orders = np.stack([order, order.T]).astype(ml_dtypes.bfloat16)
    return np.stack([high, low], axis=1), orders


def split(x):
    high = x.astype(BF16)
    return high, (x - high.astype(F32)).astype(BF16)


def dot(a, b):
    return jnp.dot(a, b, preferred_element_type=F32)


def kernel(
    obj, probe, counts, corners, amps, mats, orders,
    out, probe_out,
    ext0, ext1, ext2, win0, win1, win2, rz0, rz1, rz2, ts0, ts1, ts2, ry0, ry1, ry2,
    patch, inner, pads, sorted_amps,
    part, buf_a, sum_a, buf_b, sum_b, buf_c, sum_c, full_b, full_a, full,
    send_sem, recv_sem,
):
    ext, win, rz, ts, ry = (ext0, ext1, ext2), (win0, win1, win2), (rz0, rz1, rz2), (ts0, ts1, ts2), (ry0, ry1, ry2)
    n_row, n_col = lax.axis_size("row"), lax.axis_size("col")
    r, c = lax.axis_index("row"), lax.axis_index("col")
    z, core = r // 2, r % 2
    x, y = c // 4, c % 4
    has_row = {-1: r > 0, 1: r < n_row - 1}
    has_col = {-1: c > 0, 1: c < n_col - 1}

    yz_peers = []
    for d in range(1, 16):
        yz_peers.append((((z + d // 4) % 4) * 2 + core, x * 4 + (y + d % 4) % 4))
    x_peers = [(r, ((x + d) % 4) * 4 + y) for d in range(1, 4)]
    core_peer = (r + 1 - 2 * core, c)

    bar = pltpu.get_barrier_semaphore()

    def greet(peer):
        pl.semaphore_signal(bar, inc=1, device_id=peer, device_id_type=MESH)

    for d in (-1, 1):
        @pl.when(has_col[d])
        def _():
            greet((r, c + d))

        @pl.when(has_row[d])
        def _():
            greet((r + d, c))
    for peer in yz_peers + x_peers + [core_peer]:
        greet(peer)
    near = sum(has_row[d].astype(jnp.int32) + has_col[d].astype(jnp.int32) for d in (-1, 1))
    pl.semaphore_wait(bar, near + 19)

    sent = []
    serial = [0]

    def make(src, dst, peer, tag):
        return pltpu.make_async_remote_copy(
            src, dst, send_sem.at[tag], recv_sem.at[tag], device_id=peer, device_id_type=MESH
        )

    def launch(copy, ok=None):
        if ok is None:
            copy.start()
        else:
            @pl.when(ok)
            def _():
                copy.start()
        sent.append((copy, ok))

    def arrive(copy, ok=None):
        if ok is None:
            copy.wait_recv()
        else:
            @pl.when(ok)
            def _():
                copy.wait_recv()

    def new_tag():
        serial[0] += 1
        return serial[0] - 1

    def block(s, cb, rb):
        return ext[s].at[cb, :, pl.ds(H * rb, H), :]

    side, centre, relay = {}, {}, {}
    for s in range(SLICES):
        for d in (-1, 1):
            side[s, d] = make(obj.at[s], block(s, 1 - d, 1), (r, c + d), new_tag())
            centre[s, d] = make(obj.at[s], block(s, 1, 1 - d), (r + d, c), new_tag())
            for e in (-1, 1):
                relay[s, d, e] = make(block(s, 1 + d, 1), block(s, 1 + d, 1 - e), (r + e, c), new_tag())
    for s in range(SLICES):
        for d in (-1, 1):
            launch(side[s, d], has_col[d])
        for d in (-1, 1):
            launch(centre[s, d], has_row[d])
    for s in range(SLICES):
        ext[s][1, :, H:N, :] = obj[s]

    for q in range(CAP):
        high, low = split(amps[q])
        columns = dot(high, orders[0]) + dot(low, orders[0])
        high, low = split(columns)
        sorted_amps[q] = dot(orders[1], high) + dot(orders[1], low)
    pads[:, :, :, 0:H, :] = jnp.zeros((CAP, 3, 2, H, H), F32)
    pads[:, :, :, H + N :, :] = jnp.zeros((CAP, 3, 2, H, H), F32)

    for s in range(SLICES):
        for d in (-1, 1):
            arrive(side[s, -d], has_col[d])
            for e in (-1, 1):
                launch(relay[s, d, e], has_row[e] & has_col[d])

    base_row, base_col = r * H - H, c * H - H
    local_row = [jnp.clip(corners[q, 0] - base_row, 0, H) for q in range(CAP)]
    local_col = [jnp.clip(corners[q, 1] - base_col, 0, H) for q in range(CAP)]
    lane = lax.broadcasted_iota(jnp.int32, (N, H), 1)

    def wait_slice(s):
        for e in (-1, 1):
            arrive(centre[s, -e], has_row[e])
            for d in (-1, 1):
                arrive(relay[s, d, -e], has_row[e] & has_col[d])

    def load_patch(s):
        for q in range(CAP):
            rows = pl.ds(local_row[q], N)
            shift = lax.rem(H - local_col[q], H)
            for p in range(2):
                left, mid, right = (ext[s][cb, p, rows, :] for cb in range(3))
                patch[s, q, p, :, 0:H] = pltpu.roll(jnp.where(lane >= local_col[q], left, mid), shift, 1)
                patch[s, q, p, :, H:N] = pltpu.roll(jnp.where(lane >= local_col[q], mid, right), shift, 1)

    def times(a, b):
        return a[0] * b[0] - a[1] * b[1], a[0] * b[1] + a[1] * b[0]

    def right_product(value, which):
        high, low = split(value)
        return dot(high, mats[which, 0]) + dot(low, mats[which, 0]) + dot(high, mats[which, 1])

    def left_product(which, value):
        high, low = split(value)
        return dot(mats[which, 0], high) + dot(mats[which, 0], low) + dot(mats[which, 1], high)

    def right_halves(waves, joined):
        if joined:
            first = [[v[:, :H] + v[:, H:] for v in w] for w in waves]
            second = [[v[:, :H] - v[:, H:] for v in w] for w in waves]
        else:
            first = [[v[:, :H] for v in w] for w in waves]
            second = [[v[:, H:] for v in w] for w in waves]
        return [jnp.concatenate([jnp.concatenate(w, axis=1) for w in part_], axis=0) for part_ in (first, second)]

    def left_halves(waves, joined):
        if joined:
            first = [[v[:H] + v[H:] for v in w] for w in waves]
            second = [[v[:H] - v[H:] for v in w] for w in waves]
        else:
            first = [[v[:H] for v in w] for w in waves]
            second = [[v[H:] for v in w] for w in waves]
        return [jnp.concatenate([jnp.concatenate(w, axis=0) for w in part_], axis=1) for part_ in (first, second)]

    def right_step(waves, one, two, before, after):
        first, second = right_halves(waves, before)
        first, second = right_product(first, one), right_product(second, two)
        result = []
        for q in range(CAP):
            rows = slice(q * N, (q + 1) * N)
            pair = []
            for p in range(2):
                u, v = first[rows, p * H : (p + 1) * H], second[rows, p * H : (p + 1) * H]
                pair.append(jnp.concatenate([u + v, u - v] if after else [u, v], axis=1))
            result.append(tuple(pair))
        return result

    def left_step(waves, one, two, before, after):
        first, second = left_halves(waves, before)
        first, second = left_product(one, first), left_product(two, second)
        result = []
        for q in range(CAP):
            cols = slice(q * N, (q + 1) * N)
            pair = []
            for p in range(2):
                u, v = first[p * H : (p + 1) * H, cols], second[p * H : (p + 1) * H, cols]
                pair.append(jnp.concatenate([u + v, u - v] if after else [u, v], axis=0))
            result.append(tuple(pair))
        return result

    def prop(waves):
        return left_step(right_step(waves, FS_R, FD_R, True, True), FS_L, FD_L, True, True)

    def get_patch(s, q):
        return patch[s, q, 0], patch[s, q, 1]

    probe_pair = (probe[0], probe[1])

    wait_slice(0)
    load_patch(0)
    waves = [times(probe_pair, get_patch(0, q)) for q in range(CAP)]
    for s in range(1, SLICES):
        waves = prop(waves)
        for q in range(CAP):
            inner[s - 1, q, 0], inner[s - 1, q, 1] = waves[q]
        wait_slice(s)
        load_patch(s)
        waves = [times(waves[q], get_patch(s, q)) for q in range(CAP)]
    far = left_step(right_step(waves, E_R, O_R, True, False), E_L, O_L, True, False)
    back = []
    for q in range(CAP):
        re, im = far[q]
        live = (q < counts[0]).astype(F32)
        square = jnp.maximum(re * re + im * im, FLOOR * FLOOR)
        factor = (1.0 - sorted_amps[q] * lax.rsqrt(square)) * live
        back.append((re * factor, -(im * factor)))
    back = left_step(right_step(back, E_R, OT_R, False, True), E_L, OT_L, False, True)

    up_down = {}
    sides = {}
    for s in range(SLICES):
        for d in (-1, 1):
            up_down[s, d] = make(
                win[s].at[:, :, pl.ds(H * (1 + d), H), :], rz[s].at[(1 - d) // 2], (r + d, c), new_tag()
            )
            sides[s, d] = make(ts[s].at[(1 + d) // 2], ry[s].at[(1 - d) // 2], (r, c + d), new_tag())

    def place(s, back):
        for q in range(CAP):
            source = probe_pair if s == 0 else (inner[s - 1, q, 0], inner[s - 1, q, 1])
            re, im = times(source, back[q])
            for p, g in enumerate((re, -im)):
                one = pltpu.roll(g[:, :H], lax.rem(local_col[q], H), 1)
                two = pltpu.roll(g[:, H:], lax.rem(local_col[q], H), 1)
                high = lane >= local_col[q]
                pads[q, 0, p, H : H + N, :] = jnp.where(high, one, 0.0)
                pads[q, 1, p, H : H + N, :] = jnp.where(high, two, one)
                pads[q, 2, p, H : H + N, :] = jnp.where(high, 0.0, two)
        for cb in range(3):
            for p in range(2):
                total = pads[0, cb, p, pl.ds(H - local_row[0], 3 * H), :]
                for q in range(1, CAP):
                    total = total + pads[q, cb, p, pl.ds(H - local_row[q], 3 * H), :]
                win[s][cb, p] = total
        for d in (-1, 1):
            launch(up_down[s, d], has_row[d])

    for s in reversed(range(SLICES)):
        place(s, back)
        back = [times(get_patch(s, q), back[q]) for q in range(CAP)]
        if s > 0:
            back = prop(back)
    total_re = back[0][0] + back[1][0]
    total_im = -(back[0][1] + back[1][1])
    for p, value in enumerate((total_re, total_im)):
        for half in range(2):
            part[pl.ds((2 * p + half) * N, N), :] = value[:, half * H : (half + 1) * H]

    big, mid_rows, small = 4 * H, H, 8

    step_a = make(part.at[pl.ds((1 - core) * big, big)], buf_a, core_peer, new_tag())
    step_b = [
        make(sum_a.at[pl.ds(((x + d) % 4) * mid_rows, mid_rows)], buf_b.at[d - 1], x_peers[d - 1], new_tag())
        for d in range(1, 4)
    ]
    mine = z * 4 + y
    step_c, step_d = [], []
    for d in range(1, 16):
        theirs = ((z + d // 4) % 4) * 4 + (y + d % 4) % 4
        step_c.append(make(sum_b.at[pl.ds(theirs * small, small)], buf_c.at[d - 1], yz_peers[d - 1], new_tag()))
    for d in range(1, 16):
        step_d.append(make(sum_c, full_b.at[pl.ds(mine * small, small)], yz_peers[d - 1], new_tag()))
    step_e = [make(full_b, full_a.at[pl.ds(x * mid_rows, mid_rows)], x_peers[d - 1], new_tag()) for d in range(1, 4)]
    step_f = make(full_a, full.at[pl.ds(core * big, big)], core_peer, new_tag())

    def rows_done(s):
        for d in (-1, 1):
            arrive(up_down[s, -d], has_row[d])
        for cb in range(3):
            total = win[s][cb, :, H:N, :]
            for d in (-1, 1):
                total = total + jnp.where(has_row[d], rz[s][(1 + d) // 2, cb], 0.0)
            if cb == 1:
                out[s] = total
            else:
                ts[s][cb // 2] = total
        for d in (-1, 1):
            launch(sides[s, d], has_col[d])

    def columns_done(s):
        for d in (-1, 1):
            arrive(sides[s, -d], has_col[d])
        total = out[s]
        for d in (-1, 1):
            total = total + jnp.where(has_col[d], ry[s][(1 + d) // 2], 0.0)
        out[s] = total

    launch(step_a)
    rows_done(2)
    arrive(step_a)
    sum_a[...] = part[pl.ds(core * big, big), :] + buf_a[...]
    for copy in step_b:
        launch(copy)
    rows_done(1)
    for copy in step_b:
        arrive(copy)
    sum_b[...] = sum_a[pl.ds(x * mid_rows, mid_rows), :] + buf_b[0] + buf_b[1] + buf_b[2]
    for copy in step_c:
        launch(copy)
    columns_done(2)
    for copy in step_c:
        arrive(copy)
    total = sum_b[pl.ds(mine * small, small), :]
    for d in range(15):
        total = total + buf_c[d]
    sum_c[...] = total
    for copy in step_d:
        launch(copy)
    full_b[pl.ds(mine * small, small), :] = total
    rows_done(0)
    for copy in step_d:
        arrive(copy)
    for copy in step_e:
        launch(copy)
    full_a[pl.ds(x * mid_rows, mid_rows), :] = full_b[...]
    columns_done(1)
    for copy in step_e:
        arrive(copy)
    launch(step_f)
    full[pl.ds(core * big, big), :] = full_a[...]
    columns_done(0)
    arrive(step_f)
    for p in range(2):
        for half in range(2):
            probe_out[p, :, half * H : (half + 1) * H] = full[pl.ds((2 * p + half) * N, N), :]
    for copy, ok in sent:
        if ok is None:
            copy.wait_send()
        else:
            @pl.when(ok)
            def _():
                copy.wait_send()


N_TAGS = SLICES * 8 + SLICES * 4 + 1 + 3 + 15 + 15 + 3 + 1


def on_device(object_tiles, probe_wave, slot_counts, slot_offsets, amplitudes):
    mats, orders = constant_matrices()
    vmem = pl.BlockSpec(memory_space=pltpu.VMEM)
    smem = pl.BlockSpec(memory_space=pltpu.SMEM)
    per_slice = lambda *shape: [pltpu.VMEM(shape, F32) for _ in range(SLICES)]
    return pl.pallas_call(
        kernel,
        out_shape=(
            jax.ShapeDtypeStruct((SLICES, 2, H, H), F32),
            jax.ShapeDtypeStruct((2, N, N), F32),
        ),
        in_specs=[vmem, vmem, smem, smem, vmem, vmem, vmem],
        out_specs=(vmem, vmem),
        scratch_shapes=[
            *per_slice(3, 2, 3 * H, H),
            *per_slice(3, 2, 3 * H, H),
            *per_slice(2, 3, 2, H, H),
            *per_slice(2, 2, H, H),
            *per_slice(2, 2, H, H),
            pltpu.VMEM((SLICES, CAP, 2, N, N), F32),
            pltpu.VMEM((SLICES - 1, CAP, 2, N, N), F32),
            pltpu.VMEM((CAP, 3, 2, 2 * N, H), F32),
            pltpu.VMEM((CAP, N, N), F32),
            pltpu.VMEM((8 * H, H), F32),
            pltpu.VMEM((4 * H, H), F32),
            pltpu.VMEM((4 * H, H), F32),
            pltpu.VMEM((3, H, H), F32),
            pltpu.VMEM((H, H), F32),
            pltpu.VMEM((15, 8, H), F32),
            pltpu.VMEM((8, H), F32),
            pltpu.VMEM((H, H), F32),
            pltpu.VMEM((4 * H, H), F32),
            pltpu.VMEM((8 * H, H), F32),
            pltpu.SemaphoreType.DMA((N_TAGS,)),
            pltpu.SemaphoreType.DMA((N_TAGS,)),
        ],
        compiler_params=pltpu.CompilerParams(
            collective_id=0, has_side_effects=True, vmem_limit_bytes=60 << 20
        ),
        name="ptychography_step",
    )(
        object_tiles,
        probe_wave,
        slot_counts[0],
        slot_offsets[0, 0],
        amplitudes[0, 0],
        jnp.asarray(mats),
        jnp.asarray(orders),
    )


def solution(mesh):
    return jax.shard_map(
        on_device,
        mesh=mesh,
        in_specs=(
            P(None, None, "row", "col"),
            P(),
            P("row", "col"),
            P("row", "col", None, None),
            P("row", "col", None, None, None),
        ),
        out_specs=(P(None, None, "row", "col"), P()),
        check_vma=False,
    )
```

time: 1180 us -> 68.1 us (0.06)
  local copies, waits for them, and re-layouts: 859 us -> 3.63 us
  waiting for transfers between devices: 177 us -> 0 us
  matrix products: 69.8 us -> 0 us
  Pallas kernels: 0 us -> 62.9 us
  starting transfers between devices: 27.9 us -> 0 us
  between operations: 23 us -> 1.28 us
  other arithmetic: 13.3 us -> 0 us
    gather x5 -> x0, local copies, waits for them, and re-layouts: 813 us -> none  [fresnel_matrix(): return (real_lag[lag_index], imag_lag[lag_index])]
    psum x1 -> x0, waiting for transfers between devices: 127 us -> none  [on_device(): probe_total = lax.psum(probe_local, ('row', 'col'))]
    dot_general x52 -> x0, matrix products: 69.8 us -> none  [the longest x24 33.4 us: multiply_right(): return jnp.einsum('bjk,kl->bjl', left, right, precision=HIGHEST)]
    pallas_call x0 -> x1, Pallas kernels: none -> 62.9 us  [on_device(): pl.pallas_call(kernel, out_shape=(jax.ShapeDtypeStruct((SLICES, 2, H, H),...]
    ppermute x8 -> x0, waiting for transfers between devices: 49.8 us -> none  [the longest x4 37.9 us: padded_2(): lax.ppermute(lax.slice_in_dim(block, block.shape[dim] - width, None, axis...]
    dynamic_update_slice x2 -> x0, local copies, waits for them, and re-layouts: 37.3 us -> none  [on_device(): grad_ext = lax.dynamic_update_slice(grad_ext, piece, start)]
    ppermute x8 -> x0, starting transfers between devices: 27.9 us -> none  [the longest x4 20.8 us: padded_2(): lax.ppermute(lax.slice_in_dim(block, block.shape[dim] - width, None, axis...]
  transfers between devices with their start and end apart: 9 -> 0, of which waited for: 5 -> 0; matrix products, arithmetic and copies ran while one was open for 71% -> 0% of each run, Pallas kernels for 0% -> 0%
where the time goes in v1:
time: 68.1 us; the launch traced here: 67.9 us
  Pallas kernels  62.9 us (92%)
  local copies, waits for them, and re-layouts  3.63 us (5%)
  between operations  1.28 us (2%)
    pallas_call x1, Pallas kernels, on_device(): pl.pallas_call(kernel, out_shape=(jax.ShapeDtypeStruct((SLICES, 2, H, H),...  62.9 us
    unnamed x2, local copies, waits for them, and re-layouts  3.63 us

profile of v1, /device:TPU:1, one launch (start us, length us, event | category | flops | bytes accessed | tf_op | source)
XLA Modules:
  0.0 67.9 jit_solution(16159974645195913044)
XLA Ops:
  1.3 62.9 %ptychography_step.1 = (f32[3,2,128,128]{3,2,1,0:T(8,128)}, f32[2,256,256]{2,1,0:T(8,128)}) custom-call(f32[3,2,128,128]{3,2,1,0:T(8,128)} %obj.1, f32[2,256,256]{2,1,0:T(8,128)} %probe.1, s32[1]{0:T(128)} %bitcast.3.counts, s32[2,2]{1,0:T(2,128)} %bitcast.5, f32[2,256,256]{2,1,0:T(8,128)} %bitcast.4, bf16[10,2,256,256]{3,2,1,0:T(8,128)(2,1)} %constant.4.clone.mats, ...), custom_call_target="tpu_custom_call" | custom-call | tf_op jit(solution)/shard_map/ptychography_step/pallas_call | solution.py:406
  64.2 1.8 %copy.12 = f32[3,2,128,128]{3,2,1,0:T(8,128)} copy(f32[3,2,128,128]{3,2,1,0:T(8,128)} %get-tuple-element.4) | data formatting | bytes 786432
  66.0 1.9 %copy.13 = f32[2,256,256]{2,1,0:T(8,128)} copy(f32[2,256,256]{2,1,0:T(8,128)} %get-tuple-element.5) | data formatting | bytes 1048576

commit v2 on v1

--- a/solution.py
+++ b/solution.py
@@ -66,12 +66,13 @@
 
 
 def kernel(
-    obj, probe, counts, corners, amps, mats, orders,
+    obj, probe_hbm, counts, corners, amps_hbm, mats_hbm, orders_hbm,
     out, probe_out,
     ext0, ext1, ext2, win0, win1, win2, rz0, rz1, rz2, ts0, ts1, ts2, ry0, ry1, ry2,
     patch, inner, pads, sorted_amps,
-    part, buf_a, sum_a, buf_b, sum_b, buf_c, sum_c, full_b, full_a, full,
-    send_sem, recv_sem,
+    part, buf_a, sum_a, buf_b, sum_b, buf_c, full_a, full,
+    probe, amps, mats, orders, result, probe_result,
+    send_sem, recv_sem, load_sem, far_sem,
 ):
     ext, win, rz, ts, ry = (ext0, ext1, ext2), (win0, win1, win2), (rz0, rz1, rz2), (ts0, ts1, ts2), (ry0, ry1, ry2)
     n_row, n_col = lax.axis_size("row"), lax.axis_size("col")
@@ -81,11 +82,27 @@
     has_row = {-1: r > 0, 1: r < n_row - 1}
     has_col = {-1: c > 0, 1: c < n_col - 1}
 
-    yz_peers = []
-    for d in range(1, 16):
-        yz_peers.append((((z + d // 4) % 4) * 2 + core, x * 4 + (y + d % 4) % 4))
-    x_peers = [(r, ((x + d) % 4) * 4 + y) for d in range(1, 4)]
+    def device(dx, dy, dz):
+        return ((z + dz) % 4) * 2 + core, ((x + dx) % 4) * 4 + (y + dy) % 4
+
+    x_peers = [device(d, 0, 0) for d in range(1, 4)]
+    y_peers = [device(0, d, 0) for d in range(1, 4)]
+    z_peers = [device(0, 0, d) for d in range(1, 4)]
+    plane_peers = [device(d // 4, d % 4, 0) for d in range(1, 16)]
     core_peer = (r + 1 - 2 * core, c)
+
+    fetches = {}
+
+    def fetch(name, src, dst, place):
+        fetches[name] = pltpu.make_async_copy(src, dst, load_sem.at[place])
+        fetches[name].start()
+
+    for s in range(SLICES):
+        fetch(("obj", s), obj.at[s], (ext0, ext1, ext2)[s].at[1, :, pl.ds(H, H), :], s)
+    fetch("amps", amps_hbm.at[0, 0], amps, 3)
+    fetch("orders", orders_hbm, orders, 4)
+    fetch("probe", probe_hbm, probe, 5)
+    fetch("mats", mats_hbm, mats, 6)
 
     bar = pltpu.get_barrier_semaphore()
 
@@ -100,10 +117,10 @@
         @pl.when(has_row[d])
         def _():
             greet((r + d, c))
-    for peer in yz_peers + x_peers + [core_peer]:
+    for peer in x_peers + y_peers + z_peers:
         greet(peer)
     near = sum(has_row[d].astype(jnp.int32) + has_col[d].astype(jnp.int32) for d in (-1, 1))
-    pl.semaphore_wait(bar, near + 19)
+    pl.semaphore_wait(bar, near + 9)
 
     sent = []
     serial = [0]
@@ -149,9 +166,11 @@
             launch(side[s, d], has_col[d])
         for d in (-1, 1):
             launch(centre[s, d], has_row[d])
-    for s in range(SLICES):
-        ext[s][1, :, H:N, :] = obj[s]
-
+    for peer in y_peers:
+        pl.semaphore_signal(far_sem, inc=1, device_id=peer, device_id_type=MESH)
+
+    fetches["amps"].wait()
+    fetches["orders"].wait()
     for q in range(CAP):
         high, low = split(amps[q])
         columns = dot(high, orders[0]) + dot(low, orders[0])
@@ -167,11 +186,12 @@
                 launch(relay[s, d, e], has_row[e] & has_col[d])
 
     base_row, base_col = r * H - H, c * H - H
-    local_row = [jnp.clip(corners[q, 0] - base_row, 0, H) for q in range(CAP)]
-    local_col = [jnp.clip(corners[q, 1] - base_col, 0, H) for q in range(CAP)]
+    local_row = [jnp.clip(corners[0, 0, q, 0] - base_row, 0, H) for q in range(CAP)]
+    local_col = [jnp.clip(corners[0, 0, q, 1] - base_col, 0, H) for q in range(CAP)]
     lane = lax.broadcasted_iota(jnp.int32, (N, H), 1)
 
     def wait_slice(s):
+        fetches["obj", s].wait()
         for e in (-1, 1):
             arrive(centre[s, -e], has_row[e])
             for d in (-1, 1):
@@ -247,7 +267,9 @@
     def get_patch(s, q):
         return patch[s, q, 0], patch[s, q, 1]
 
+    fetches["probe"].wait()
     probe_pair = (probe[0], probe[1])
+    fetches["mats"].wait()
 
     wait_slice(0)
     load_patch(0)
@@ -263,7 +285,7 @@
     back = []
     for q in range(CAP):
         re, im = far[q]
-        live = (q < counts[0]).astype(F32)
+        live = (q < counts[0, 0]).astype(F32)
         square = jnp.maximum(re * re + im * im, FLOOR * FLOOR)
         factor = (1.0 - sorted_amps[q] * lax.rsqrt(square)) * live
         back.append((re * factor, -(im * factor)))
@@ -298,8 +320,28 @@
         for d in (-1, 1):
             launch(up_down[s, d], has_row[d])
 
+    big, small = 4 * H, 4 * H // 16
+    step_a = make(part.at[pl.ds((1 - core) * big, big)], buf_a, core_peer, new_tag())
+    step_b, step_c, step_d, step_e = [], [], [], []
+    for d in range(1, 16):
+        theirs = ((x + d // 4) % 4) * 4 + (y + d % 4) % 4
+        step_b.append(make(sum_a.at[pl.ds(theirs * small, small)], buf_b.at[d - 1], plane_peers[d - 1], new_tag()))
+    for d in range(1, 4):
+        step_c.append(make(sum_b, buf_c.at[d - 1], z_peers[d - 1], new_tag()))
+    own_rows = pl.ds(c * small, small)
+    for d in range(1, 16):
+        step_d.append(make(full_a.at[own_rows], full_a.at[own_rows], plane_peers[d - 1], new_tag()))
+    for d in range(4):
+        rows = ((x - d + 4) % 4) * 4 * small
+        step_e.append(
+            make(full_a.at[pl.ds(rows, 4 * small)], full.at[pl.ds(core * big + rows, 4 * small)], core_peer, new_tag())
+        )
+
+    backs = {}
     for s in reversed(range(SLICES)):
-        place(s, back)
+        backs[s] = back
+        if s == SLICES - 1:
+            place(s, back)
         back = [times(get_patch(s, q), back[q]) for q in range(CAP)]
         if s > 0:
             back = prop(back)
@@ -308,23 +350,8 @@
     for p, value in enumerate((total_re, total_im)):
         for half in range(2):
             part[pl.ds((2 * p + half) * N, N), :] = value[:, half * H : (half + 1) * H]
-
-    big, mid_rows, small = 4 * H, H, 8
-
-    step_a = make(part.at[pl.ds((1 - core) * big, big)], buf_a, core_peer, new_tag())
-    step_b = [
-        make(sum_a.at[pl.ds(((x + d) % 4) * mid_rows, mid_rows)], buf_b.at[d - 1], x_peers[d - 1], new_tag())
-        for d in range(1, 4)
-    ]
-    mine = z * 4 + y
-    step_c, step_d = [], []
-    for d in range(1, 16):
-        theirs = ((z + d // 4) % 4) * 4 + (y + d % 4) % 4
-        step_c.append(make(sum_b.at[pl.ds(theirs * small, small)], buf_c.at[d - 1], yz_peers[d - 1], new_tag()))
-    for d in range(1, 16):
-        step_d.append(make(sum_c, full_b.at[pl.ds(mine * small, small)], yz_peers[d - 1], new_tag()))
-    step_e = [make(full_b, full_a.at[pl.ds(x * mid_rows, mid_rows)], x_peers[d - 1], new_tag()) for d in range(1, 4)]
-    step_f = make(full_a, full.at[pl.ds(core * big, big)], core_peer, new_tag())
+    launch(step_a)
+    pl.semaphore_wait(far_sem, 3)
 
     def rows_done(s):
         for d in (-1, 1):
@@ -334,7 +361,7 @@
             for d in (-1, 1):
                 total = total + jnp.where(has_row[d], rz[s][(1 + d) // 2, cb], 0.0)
             if cb == 1:
-                out[s] = total
+                result[s] = total
             else:
                 ts[s][cb // 2] = total
         for d in (-1, 1):
@@ -343,49 +370,62 @@
     def columns_done(s):
         for d in (-1, 1):
             arrive(sides[s, -d], has_col[d])
-        total = out[s]
+        total = result[s]
         for d in (-1, 1):
             total = total + jnp.where(has_col[d], ry[s][(1 + d) // 2], 0.0)
-        out[s] = total
-
-    launch(step_a)
-    rows_done(2)
+        result[s] = total
+        fetch(("out", s), result.at[s], out.at[s], 7 + s)
+
     arrive(step_a)
     sum_a[...] = part[pl.ds(core * big, big), :] + buf_a[...]
     for copy in step_b:
         launch(copy)
-    rows_done(1)
+    place(1, backs[1])
+    place(0, backs[0])
+    rows_done(2)
     for copy in step_b:
         arrive(copy)
-    sum_b[...] = sum_a[pl.ds(x * mid_rows, mid_rows), :] + buf_b[0] + buf_b[1] + buf_b[2]
+    total = sum_a[own_rows, :]
+    for d in range(15):
+        total = total + buf_b[d]
+    sum_b[...] = total
     for copy in step_c:
         launch(copy)
-    columns_done(2)
+    rows_done(1)
     for copy in step_c:
         arrive(copy)
-    total = sum_b[pl.ds(mine * small, small), :]
-    for d in range(15):
-        total = total + buf_c[d]
-    sum_c[...] = total
+    full_a[own_rows, :] = sum_b[...] + buf_c[0] + buf_c[1] + buf_c[2]
     for copy in step_d:
         launch(copy)
-    full_b[pl.ds(mine * small, small), :] = total
+    columns_done(2)
     rows_done(0)
-    for copy in step_d:
-        arrive(copy)
-    for copy in step_e:
-        launch(copy)
-    full_a[pl.ds(x * mid_rows, mid_rows), :] = full_b[...]
     columns_done(1)
+    for d in range(4):
+        for k in range(4):
+            if 4 * d + k > 0:
+                arrive(step_d[4 * d + k - 1])
+        launch(step_e[d])
+    own_half = [pltpu.make_async_copy(probe_result.at[p], probe_out.at[p], load_sem.at[10]) for p in range(2)]
+    other_half = [pltpu.make_async_copy(probe_result.at[p], probe_out.at[p], load_sem.at[11]) for p in range(2)]
+    for p in range(2):
+        @pl.when(core == p)
+        def _():
+            for half in range(2):
+                probe_result[p, :, half * H : (half + 1) * H] = full_a[pl.ds(half * N, N), :]
+            own_half[p].start()
+    columns_done(0)
     for copy in step_e:
         arrive(copy)
-    launch(step_f)
-    full[pl.ds(core * big, big), :] = full_a[...]
-    columns_done(0)
-    arrive(step_f)
     for p in range(2):
-        for half in range(2):
-            probe_out[p, :, half * H : (half + 1) * H] = full[pl.ds((2 * p + half) * N, N), :]
+        @pl.when(core != p)
+        def _():
+            for half in range(2):
+                probe_result[p, :, half * H : (half + 1) * H] = full[pl.ds((2 * p + half) * N, N), :]
+            other_half[p].start()
+    own_half[0].wait()
+    other_half[0].wait()
+    for s in range(SLICES):
+        fetches["out", s].wait()
     for copy, ok in sent:
         if ok is None:
             copy.wait_send()
@@ -395,22 +435,34 @@
                 copy.wait_send()
 
 
-N_TAGS = SLICES * 8 + SLICES * 4 + 1 + 3 + 15 + 15 + 3 + 1
+N_TAGS = SLICES * 8 + SLICES * 4 + 1 + 15 + 3 + 15 + 4
+
+
+def finish(grad, probe_grad, out, probe_out, held, probe_held, sem):
+    places = [(grad.at[s], held.at[s], out.at[s]) for s in range(SLICES)]
+    places += [(probe_grad.at[p], probe_held.at[p], probe_out.at[p]) for p in range(2)]
+    loads = [pltpu.make_async_copy(a, b, sem.at[0, i]) for i, (a, b, _) in enumerate(places)]
+    stores = [pltpu.make_async_copy(b, c, sem.at[1, i]) for i, (_, b, c) in enumerate(places)]
+    for copy in loads:
+        copy.start()
+    for load, store in zip(loads, stores):
+        load.wait()
+        store.start()
+    for copy in stores:
+        copy.wait()
 
 
 def on_device(object_tiles, probe_wave, slot_counts, slot_offsets, amplitudes):
     mats, orders = constant_matrices()
-    vmem = pl.BlockSpec(memory_space=pltpu.VMEM)
     smem = pl.BlockSpec(memory_space=pltpu.SMEM)
     per_slice = lambda *shape: [pltpu.VMEM(shape, F32) for _ in range(SLICES)]
-    return pl.pallas_call(
+    shapes = (jax.ShapeDtypeStruct((SLICES, 2, H, H), F32), jax.ShapeDtypeStruct((2, N, N), F32))
+    hbm = pl.BlockSpec(memory_space=pl.ANY)
+    grads = pl.pallas_call(
         kernel,
-        out_shape=(
-            jax.ShapeDtypeStruct((SLICES, 2, H, H), F32),
-            jax.ShapeDtypeStruct((2, N, N), F32),
-        ),
-        in_specs=[vmem, vmem, smem, smem, vmem, vmem, vmem],
-        out_specs=(vmem, vmem),
+        out_shape=shapes,
+        in_specs=[hbm, hbm, smem, smem, hbm, hbm, hbm],
+        out_specs=(hbm, hbm),
         scratch_shapes=[
             *per_slice(3, 2, 3 * H, H),
             *per_slice(3, 2, 3 * H, H),
@@ -424,15 +476,21 @@
             pltpu.VMEM((8 * H, H), F32),
             pltpu.VMEM((4 * H, H), F32),
             pltpu.VMEM((4 * H, H), F32),
-            pltpu.VMEM((3, H, H), F32),
-            pltpu.VMEM((H, H), F32),
-            pltpu.VMEM((15, 8, H), F32),
-            pltpu.VMEM((8, H), F32),
-            pltpu.VMEM((H, H), F32),
+            pltpu.VMEM((15, 4 * H // 16, H), F32),
+            pltpu.VMEM((4 * H // 16, H), F32),
+            pltpu.VMEM((3, 4 * H // 16, H), F32),
             pltpu.VMEM((4 * H, H), F32),
             pltpu.VMEM((8 * H, H), F32),
+            pltpu.VMEM((2, N, N), F32),
+            pltpu.VMEM((CAP, N, N), F32),
+            pltpu.VMEM((10, 2, N, N), BF16),
+            pltpu.VMEM((2, N, N), BF16),
+            pltpu.VMEM((SLICES, 2, H, H), F32),
+            pltpu.VMEM((2, N, N), F32),
             pltpu.SemaphoreType.DMA((N_TAGS,)),
             pltpu.SemaphoreType.DMA((N_TAGS,)),
+            pltpu.SemaphoreType.DMA((12,)),
+            pltpu.SemaphoreType.REGULAR,
         ],
         compiler_params=pltpu.CompilerParams(
             collective_id=0, has_side_effects=True, vmem_limit_bytes=60 << 20
@@ -441,12 +499,24 @@
     )(
         object_tiles,
         probe_wave,
-        slot_counts[0],
-        slot_offsets[0, 0],
-        amplitudes[0, 0],
+        slot_counts,
+        slot_offsets,
+        amplitudes,
         jnp.asarray(mats),
         jnp.asarray(orders),
     )
+    return pl.pallas_call(
+        finish,
+        out_shape=shapes,
+        in_specs=[hbm, hbm],
+        out_specs=(hbm, hbm),
+        scratch_shapes=[
+            pltpu.VMEM((SLICES, 2, H, H), F32),
+            pltpu.VMEM((2, N, N), F32),
+            pltpu.SemaphoreType.DMA((2, SLICES + 2)),
+        ],
+        name="results",
+    )(*grads)
 
 
 def solution(mesh):

time: 68.1 us -> 57.3 us (0.84)
  Pallas kernels: 62.9 us -> 55.6 us
  local copies, waits for them, and re-layouts: 3.63 us -> 0 us
    pallas_call x1 -> x2, Pallas kernels: 62.9 us -> 55.6 us  [the longest x1 53.6 us: on_device(): pl.pallas_call(kernel, out_shape=shapes, in_specs=[hbm, hbm, smem, smem,...]
    unnamed x2 -> x0, local copies, waits for them, and re-layouts: 3.63 us -> none
where the time goes in v2:
time: 57.3 us; the launch traced here: 56.9 us
  Pallas kernels  55.6 us (97%)
  between operations  1.28 us (2%)
    pallas_call x1, Pallas kernels, on_device(): pl.pallas_call(kernel, out_shape=shapes, in_specs=[hbm, hbm, smem, smem,...  53.6 us
    pallas_call x1, Pallas kernels, on_device(): pl.pallas_call(finish, out_shape=shapes, in_specs=[hbm, hbm], out_specs=(...  2.02 us

profile of v2, /device:TPU:1, one launch (start us, length us, event | category | flops | bytes accessed | tf_op | source)
XLA Modules:
  0.0 56.9 jit_solution(3864350579245428015)
XLA Ops:
  1.3 53.6 %ptychography_step.1 = (f32[3,2,128,128]{3,2,1,0:T(8,128)}, f32[2,256,256]{2,1,0:T(8,128)}) custom-call(f32[3,2,128,128]{3,2,1,0:T(8,128)} %obj.1, f32[2,256,256]{2,1,0:T(8,128)} %probe_hbm.1, s32[1,1]{1,0:T(1,128)S(6)} %copy.9.counts, s32[1,1,2,2]{3,2,1,0:T(2,128)} %corners.1, f32[1,1,2,256,256]{4,3,2,1,0:T(8,128)} %amps_hbm.1, ...), custom_call_target="tpu_custom_call" | custom-call | tf_op jit(solution)/shard_map/ptychography_step/pallas_call | solution.py:461
  54.9 2.0 %results.1 = (f32[3,2,128,128]{3,2,1,0:T(8,128)}, f32[2,256,256]{2,1,0:T(8,128)}) custom-call(f32[3,2,128,128]{3,2,1,0:T(8,128)} %get-tuple-element.4.grad, f32[2,256,256]{2,1,0:T(8,128)} %get-tuple-element.5.probe_grad), custom_call_target="tpu_custom_call" | custom-call | tf_op jit(solution)/shard_map/results/pallas_call | solution.py:508

commit v3 on v2

--- a/solution.py
+++ b/solution.py
@@ -70,9 +70,9 @@
     out, probe_out,
     ext0, ext1, ext2, win0, win1, win2, rz0, rz1, rz2, ts0, ts1, ts2, ry0, ry1, ry2,
     patch, inner, pads, sorted_amps,
-    part, buf_a, sum_a, buf_b, sum_b, buf_c, full_a, full,
+    corner_in, corner_sum, part, buf_a, sum_a, buf_b, full_a, full,
     probe, amps, mats, orders, result, probe_result,
-    send_sem, recv_sem, load_sem, far_sem,
+    send_sem, recv_sem, load_sem, plane_sem, far_sem,
 ):
     ext, win, rz, ts, ry = (ext0, ext1, ext2), (win0, win1, win2), (rz0, rz1, rz2), (ts0, ts1, ts2), (ry0, ry1, ry2)
     n_row, n_col = lax.axis_size("row"), lax.axis_size("col")
@@ -88,7 +88,8 @@
     x_peers = [device(d, 0, 0) for d in range(1, 4)]
     y_peers = [device(0, d, 0) for d in range(1, 4)]
     z_peers = [device(0, 0, d) for d in range(1, 4)]
-    plane_peers = [device(d // 4, d % 4, 0) for d in range(1, 16)]
+    offsets = [(d // 16, d // 4 % 4, d % 4) for d in range(1, 64)]
+    offsets.sort(key=lambda steps: -sum(min(v, 4 - v) for v in steps))
     core_peer = (r + 1 - 2 * core, c)
 
     fetches = {}
@@ -154,20 +155,33 @@
     def block(s, cb, rb):
         return ext[s].at[cb, :, pl.ds(H * rb, H), :]
 
-    side, centre, relay = {}, {}, {}
+    on_chip = {1: core == 0, -1: core == 1}
+    across = {1: core == 1, -1: core == 0}
+    has_across = (has_row[-1] & across[-1]) | (has_row[1] & across[1])
+    across_rows = pl.ds(core * N, H)
+
+    side, centre, relay, corner = {}, {}, {}, {}
     for s in range(SLICES):
         for d in (-1, 1):
             side[s, d] = make(obj.at[s], block(s, 1 - d, 1), (r, c + d), new_tag())
             centre[s, d] = make(obj.at[s], block(s, 1, 1 - d), (r + d, c), new_tag())
             for e in (-1, 1):
                 relay[s, d, e] = make(block(s, 1 + d, 1), block(s, 1 + d, 1 - e), (r + e, c), new_tag())
+    for d in (-1, 1):
+        corner[d] = make(
+            ext[SLICES - 1].at[1, :, across_rows, :], ext[SLICES - 1].at[1 - d, :, across_rows, :], (r, c + d), new_tag()
+        )
+
+    def relayed(s, e):
+        return has_row[e] & on_chip[e] if s == SLICES - 1 else has_row[e]
+
     for s in range(SLICES):
         for d in (-1, 1):
             launch(side[s, d], has_col[d])
         for d in (-1, 1):
             launch(centre[s, d], has_row[d])
     for peer in y_peers:
-        pl.semaphore_signal(far_sem, inc=1, device_id=peer, device_id_type=MESH)
+        pl.semaphore_signal(plane_sem, inc=1, device_id=peer, device_id_type=MESH)
 
     fetches["amps"].wait()
     fetches["orders"].wait()
@@ -179,11 +193,20 @@
     pads[:, :, :, 0:H, :] = jnp.zeros((CAP, 3, 2, H, H), F32)
     pads[:, :, :, H + N :, :] = jnp.zeros((CAP, 3, 2, H, H), F32)
 
+    pl.semaphore_wait(plane_sem, 3)
+    for peer in z_peers:
+        pl.semaphore_signal(far_sem, inc=1, device_id=peer, device_id_type=MESH)
+
     for s in range(SLICES):
         for d in (-1, 1):
             arrive(side[s, -d], has_col[d])
             for e in (-1, 1):
-                launch(relay[s, d, e], has_row[e] & has_col[d])
+                launch(relay[s, d, e], relayed(s, e) & has_col[d])
+        if s == SLICES - 2:
+            for e in (-1, 1):
+                arrive(centre[SLICES - 1, -e], has_row[e])
+            for d in (-1, 1):
+                launch(corner[d], has_across & has_col[d])
 
     base_row, base_col = r * H - H, c * H - H
     local_row = [jnp.clip(corners[0, 0, q, 0] - base_row, 0, H) for q in range(CAP)]
@@ -193,9 +216,13 @@
     def wait_slice(s):
         fetches["obj", s].wait()
         for e in (-1, 1):
-            arrive(centre[s, -e], has_row[e])
+            if s < SLICES - 1:
+                arrive(centre[s, -e], has_row[e])
             for d in (-1, 1):
-                arrive(relay[s, d, -e], has_row[e] & has_col[d])
+                arrive(relay[s, d, -e], relayed(s, e) & has_col[d])
+        if s == SLICES - 1:
+            for d in (-1, 1):
+                arrive(corner[-d], has_across & has_col[d])
 
     def load_patch(s):
         for q in range(CAP):
@@ -300,6 +327,12 @@
             )
             sides[s, d] = make(ts[s].at[(1 + d) // 2], ry[s].at[(1 - d) // 2], (r, c + d), new_tag())
 
+    corner_back = {
+        d: make(win[0].at[1 + d, :, across_rows, :], corner_in.at[(1 - d) // 2], (r, c + d), new_tag()) for d in (-1, 1)
+    }
+    far_row = (r + 2 * core - 1, c)
+    centre_back = make(corner_sum, rz[0].at[1 - core, 1], far_row, new_tag())
+
     def place(s, back):
         for q in range(CAP):
             source = probe_pair if s == 0 else (inner[s - 1, q, 0], inner[s - 1, q, 1])
@@ -318,24 +351,32 @@
                     total = total + pads[q, cb, p, pl.ds(H - local_row[q], 3 * H), :]
                 win[s][cb, p] = total
         for d in (-1, 1):
-            launch(up_down[s, d], has_row[d])
-
-    big, small = 4 * H, 4 * H // 16
+            launch(up_down[s, d], has_row[d] & on_chip[d] if s == 0 else has_row[d])
+        if s == 0:
+            for d in (-1, 1):
+                launch(corner_back[d], has_across & has_col[d])
+
+    def corners_done():
+        for d in (-1, 1):
+            arrive(corner_back[-d], has_across & has_col[d])
+        total = win[0][1, :, across_rows, :]
+        for d in (-1, 1):
+            total = total + jnp.where(has_col[d], corner_in[(1 + d) // 2], 0.0)
+        corner_sum[...] = total
+        launch(centre_back, has_across)
+
+    big, small = 4 * H, 4 * H // 64
     step_a = make(part.at[pl.ds((1 - core) * big, big)], buf_a, core_peer, new_tag())
-    step_b, step_c, step_d, step_e = [], [], [], []
-    for d in range(1, 16):
-        theirs = ((x + d // 4) % 4) * 4 + (y + d % 4) % 4
-        step_b.append(make(sum_a.at[pl.ds(theirs * small, small)], buf_b.at[d - 1], plane_peers[d - 1], new_tag()))
-    for d in range(1, 4):
-        step_c.append(make(sum_b, buf_c.at[d - 1], z_peers[d - 1], new_tag()))
-    own_rows = pl.ds(c * small, small)
-    for d in range(1, 16):
-        step_d.append(make(full_a.at[own_rows], full_a.at[own_rows], plane_peers[d - 1], new_tag()))
-    for d in range(4):
-        rows = ((x - d + 4) % 4) * 4 * small
-        step_e.append(
-            make(full_a.at[pl.ds(rows, 4 * small)], full.at[pl.ds(core * big + rows, 4 * small)], core_peer, new_tag())
-        )
+    own_rows = pl.ds((z * 16 + c) * small, small)
+    out_tag, back_tag = new_tag(), new_tag()
+    step_b, step_c = [], []
+    for at, (dz, dx, dy) in enumerate(offsets):
+        theirs = (z + dz) % 4 * 16 + (x + dx) % 4 * 4 + (y + dy) % 4
+        step_b.append(make(sum_a.at[pl.ds(theirs * small, small)], buf_b.at[at], device(dx, dy, dz), out_tag))
+        step_c.append(make(full_a.at[own_rows], full_a.at[own_rows], device(dx, dy, dz), back_tag))
+    all_b = make(buf_b, buf_b, core_peer, out_tag)
+    all_c = make(full_a.at[pl.ds(0, 63 * small)], full_a.at[pl.ds(0, 63 * small)], core_peer, back_tag)
+    step_d = make(full_a, full.at[pl.ds(core * big, big)], core_peer, new_tag())
 
     backs = {}
     for s in reversed(range(SLICES)):
@@ -355,11 +396,14 @@
 
     def rows_done(s):
         for d in (-1, 1):
-            arrive(up_down[s, -d], has_row[d])
+            arrive(up_down[s, -d], has_row[d] & on_chip[d] if s == 0 else has_row[d])
+        if s == 0:
+            arrive(centre_back, has_across)
         for cb in range(3):
             total = win[s][cb, :, H:N, :]
             for d in (-1, 1):
-                total = total + jnp.where(has_row[d], rz[s][(1 + d) // 2, cb], 0.0)
+                whole = s > 0 or cb == 1
+                total = total + jnp.where(has_row[d] if whole else on_chip[d], rz[s][(1 + d) // 2, cb], 0.0)
             if cb == 1:
                 result[s] = total
             else:
@@ -379,32 +423,24 @@
     arrive(step_a)
     sum_a[...] = part[pl.ds(core * big, big), :] + buf_a[...]
     for copy in step_b:
-        launch(copy)
+        copy.start()
     place(1, backs[1])
     place(0, backs[0])
     rows_done(2)
-    for copy in step_b:
-        arrive(copy)
+    all_b.wait_recv()
     total = sum_a[own_rows, :]
-    for d in range(15):
+    for d in range(63):
         total = total + buf_b[d]
-    sum_b[...] = total
+    full_a[own_rows, :] = total
     for copy in step_c:
-        launch(copy)
+        copy.start()
+    corners_done()
+    columns_done(2)
     rows_done(1)
-    for copy in step_c:
-        arrive(copy)
-    full_a[own_rows, :] = sum_b[...] + buf_c[0] + buf_c[1] + buf_c[2]
-    for copy in step_d:
-        launch(copy)
-    columns_done(2)
     rows_done(0)
     columns_done(1)
-    for d in range(4):
-        for k in range(4):
-            if 4 * d + k > 0:
-                arrive(step_d[4 * d + k - 1])
-        launch(step_e[d])
+    all_c.wait_recv()
+    launch(step_d)
     own_half = [pltpu.make_async_copy(probe_result.at[p], probe_out.at[p], load_sem.at[10]) for p in range(2)]
     other_half = [pltpu.make_async_copy(probe_result.at[p], probe_out.at[p], load_sem.at[11]) for p in range(2)]
     for p in range(2):
@@ -414,8 +450,7 @@
                 probe_result[p, :, half * H : (half + 1) * H] = full_a[pl.ds(half * N, N), :]
             own_half[p].start()
     columns_done(0)
-    for copy in step_e:
-        arrive(copy)
+    arrive(step_d)
     for p in range(2):
         @pl.when(core != p)
         def _():
@@ -426,6 +461,8 @@
     other_half[0].wait()
     for s in range(SLICES):
         fetches["out", s].wait()
+    all_b.wait_send()
+    all_c.wait_send()
     for copy, ok in sent:
         if ok is None:
             copy.wait_send()
@@ -435,7 +472,7 @@
                 copy.wait_send()
 
 
-N_TAGS = SLICES * 8 + SLICES * 4 + 1 + 15 + 3 + 15 + 4
+N_TAGS = SLICES * 8 + 2 + SLICES * 4 + 3 + 1 + 2 + 1
 
 
 def finish(grad, probe_grad, out, probe_out, held, probe_held, sem):
@@ -473,12 +510,12 @@
             pltpu.VMEM((SLICES - 1, CAP, 2, N, N), F32),
             pltpu.VMEM((CAP, 3, 2, 2 * N, H), F32),
             pltpu.VMEM((CAP, N, N), F32),
+            pltpu.VMEM((2, 2, H, H), F32),
+            pltpu.VMEM((2, H, H), F32),
             pltpu.VMEM((8 * H, H), F32),
             pltpu.VMEM((4 * H, H), F32),
             pltpu.VMEM((4 * H, H), F32),
-            pltpu.VMEM((15, 4 * H // 16, H), F32),
-            pltpu.VMEM((4 * H // 16, H), F32),
-            pltpu.VMEM((3, 4 * H // 16, H), F32),
+            pltpu.VMEM((63, 4 * H // 64, H), F32),
             pltpu.VMEM((4 * H, H), F32),
             pltpu.VMEM((8 * H, H), F32),
             pltpu.VMEM((2, N, N), F32),
@@ -490,6 +527,7 @@
             pltpu.SemaphoreType.DMA((N_TAGS,)),
             pltpu.SemaphoreType.DMA((N_TAGS,)),
             pltpu.SemaphoreType.DMA((12,)),
+            pltpu.SemaphoreType.REGULAR,
             pltpu.SemaphoreType.REGULAR,
         ],
         compiler_params=pltpu.CompilerParams(

time: 57.3 us -> 53.6 us (0.935)
  the two profiles are of different devices: /device:TPU:1 before, /device:TPU:34 now
where the time goes in v3:
time: 53.6 us; the launch traced here: 53.5 us
  Pallas kernels  52.2 us (97%)
  between operations  1.28 us (2%)
    pallas_call x1, Pallas kernels, on_device(): pl.pallas_call(kernel, out_shape=shapes, in_specs=[hbm, hbm, smem, smem,...  50.2 us
    pallas_call x1, Pallas kernels, on_device(): pl.pallas_call(finish, out_shape=shapes, in_specs=[hbm, hbm], out_specs=(...  2.02 us

profile of v3, /device:TPU:34, one launch (start us, length us, event | category | flops | bytes accessed | tf_op | source)
XLA Modules:
  0.0 53.5 jit_solution(4689990792049030106)
XLA Ops:
  1.3 50.2 %ptychography_step.1 = (f32[3,2,128,128]{3,2,1,0:T(8,128)}, f32[2,256,256]{2,1,0:T(8,128)}) custom-call(f32[3,2,128,128]{3,2,1,0:T(8,128)} %obj.1, f32[2,256,256]{2,1,0:T(8,128)} %probe_hbm.1, s32[1,1]{1,0:T(1,128)S(6)} %copy.9.counts, s32[1,1,2,2]{3,2,1,0:T(2,128)} %corners.1, f32[1,1,2,256,256]{4,3,2,1,0:T(8,128)} %amps_hbm.1, ...), custom_call_target="tpu_custom_call" | custom-call | tf_op jit(solution)/shard_map/ptychography_step/pallas_call | solution.py:498
  51.5 2.0 %results.1 = (f32[3,2,128,128]{3,2,1,0:T(8,128)}, f32[2,256,256]{2,1,0:T(8,128)}) custom-call(f32[3,2,128,128]{3,2,1,0:T(8,128)} %get-tuple-element.4.grad, f32[2,256,256]{2,1,0:T(8,128)} %get-tuple-element.5.probe_grad), custom_call_target="tpu_custom_call" | custom-call | tf_op jit(solution)/shard_map/results/pallas_call | solution.py:546

commit v4 on v3

--- a/solution.py
+++ b/solution.py
@@ -66,12 +66,12 @@
 
 
 def kernel(
-    obj, probe_hbm, counts, corners, amps_hbm, mats_hbm, orders_hbm,
+    obj, probe_hbm, counts_hbm, corners_hbm, amps_hbm, mats_hbm, orders_hbm,
     out, probe_out,
     ext0, ext1, ext2, win0, win1, win2, rz0, rz1, rz2, ts0, ts1, ts2, ry0, ry1, ry2,
     patch, inner, pads, sorted_amps,
     corner_in, corner_sum, part, buf_a, sum_a, buf_b, full_a, full,
-    probe, amps, mats, orders, result, probe_result,
+    probe, amps, mats, orders, result, counts, corners,
     send_sem, recv_sem, load_sem, plane_sem, far_sem,
 ):
     ext, win, rz, ts, ry = (ext0, ext1, ext2), (win0, win1, win2), (rz0, rz1, rz2), (ts0, ts1, ts2), (ry0, ry1, ry2)
@@ -88,8 +88,9 @@
     x_peers = [device(d, 0, 0) for d in range(1, 4)]
     y_peers = [device(0, d, 0) for d in range(1, 4)]
     z_peers = [device(0, 0, d) for d in range(1, 4)]
+    planes = (2, 1, 3, 0)
     offsets = [(d // 16, d // 4 % 4, d % 4) for d in range(1, 64)]
-    offsets.sort(key=lambda steps: -sum(min(v, 4 - v) for v in steps))
+    offsets.sort(key=lambda steps: (planes.index(steps[0]), -sum(min(v, 4 - v) for v in steps)))
     core_peer = (r + 1 - 2 * core, c)
 
     fetches = {}
@@ -100,6 +101,8 @@
 
     for s in range(SLICES):
         fetch(("obj", s), obj.at[s], (ext0, ext1, ext2)[s].at[1, :, pl.ds(H, H), :], s)
+    fetch("counts", counts_hbm, counts, 18)
+    fetch("corners", corners_hbm, corners, 19)
     fetch("amps", amps_hbm.at[0, 0], amps, 3)
     fetch("orders", orders_hbm, orders, 4)
     fetch("probe", probe_hbm, probe, 5)
@@ -123,12 +126,15 @@
     near = sum(has_row[d].astype(jnp.int32) + has_col[d].astype(jnp.int32) for d in (-1, 1))
     pl.semaphore_wait(bar, near + 9)
 
-    sent = []
     serial = [0]
 
-    def make(src, dst, peer, tag):
+    groups = {}
+
+    def make(src, dst, peer, tag, group, ok=None, amount=0.0):
+        entry = groups.setdefault(group, [len(groups), ok, 0.0])
+        entry[2] += amount
         return pltpu.make_async_remote_copy(
-            src, dst, send_sem.at[tag], recv_sem.at[tag], device_id=peer, device_id_type=MESH
+            src, dst, send_sem.at[entry[0]], recv_sem.at[tag], device_id=peer, device_id_type=MESH
         )
 
     def launch(copy, ok=None):
@@ -138,7 +144,6 @@
             @pl.when(ok)
             def _():
                 copy.start()
-        sent.append((copy, ok))
 
     def arrive(copy, ok=None):
         if ok is None:
@@ -161,25 +166,51 @@
     across_rows = pl.ds(core * N, H)
 
     side, centre, relay, corner = {}, {}, {}, {}
+    halves = [(s, p, 1) for s in range(SLICES - 1) for p in range(2)] + [(SLICES - 1, 0, 2)]
+
+    def half_block(s, p, n, cb, rb):
+        return ext[s].at[cb, pl.ds(p, n), pl.ds(H * rb, H), :]
+
+    def relayed(s, e):
+        return has_row[e] & on_chip[e] if s == SLICES - 1 else has_row[e]
+
+    rows_tag = {(s, e): new_tag() for s in range(SLICES) for e in (-1, 1)}
     for s in range(SLICES):
         for d in (-1, 1):
-            side[s, d] = make(obj.at[s], block(s, 1 - d, 1), (r, c + d), new_tag())
-            centre[s, d] = make(obj.at[s], block(s, 1, 1 - d), (r + d, c), new_tag())
+            tag = new_tag() if s == SLICES - 1 else rows_tag[s, d]
+            centre[s, d] = make(obj.at[s], block(s, 1, 1 - d), (r + d, c), tag, ("row", d), has_row[d], 1)
+    for s, p, n in halves:
+        for d in (-1, 1):
+            side[s, p, d] = make(
+                obj.at[s, pl.ds(p, n)], half_block(s, p, n, 1 - d, 1), (r, c + d), new_tag(), ("col", d), has_col[d], n / 2
+            )
             for e in (-1, 1):
-                relay[s, d, e] = make(block(s, 1 + d, 1), block(s, 1 + d, 1 - e), (r + e, c), new_tag())
+                relay[s, p, d, e] = make(
+                    half_block(s, p, n, 1 + d, 1),
+                    half_block(s, p, n, 1 + d, 1 - e),
+                    (r + e, c),
+                    rows_tag[s, e],
+                    ("relay", s == SLICES - 1, d, e),
+                    relayed(s, e) & has_col[d],
+                    n / 2,
+                )
     for d in (-1, 1):
         corner[d] = make(
-            ext[SLICES - 1].at[1, :, across_rows, :], ext[SLICES - 1].at[1 - d, :, across_rows, :], (r, c + d), new_tag()
+            ext[SLICES - 1].at[1, :, across_rows, :],
+            ext[SLICES - 1].at[1 - d, :, across_rows, :],
+            (r, c + d),
+            new_tag(),
+            ("corner", d),
+            has_across & has_col[d],
+            1,
         )
 
-    def relayed(s, e):
-        return has_row[e] & on_chip[e] if s == SLICES - 1 else has_row[e]
-
-    for s in range(SLICES):
-        for d in (-1, 1):
-            launch(side[s, d], has_col[d])
-        for d in (-1, 1):
-            launch(centre[s, d], has_row[d])
+    for s, p, n in halves:
+        for d in (-1, 1):
+            launch(side[s, p, d], has_col[d])
+        if p == 0:
+            for d in (-1, 1):
+                launch(centre[s, d], has_row[d])
     for peer in y_peers:
         pl.semaphore_signal(plane_sem, inc=1, device_id=peer, device_id_type=MESH)
 
@@ -197,29 +228,43 @@
     for peer in z_peers:
         pl.semaphore_signal(far_sem, inc=1, device_id=peer, device_id_type=MESH)
 
-    for s in range(SLICES):
-        for d in (-1, 1):
-            arrive(side[s, -d], has_col[d])
+    for s, p, n in halves:
+        if s == SLICES - 1:
             for e in (-1, 1):
-                launch(relay[s, d, e], relayed(s, e) & has_col[d])
-        if s == SLICES - 2:
-            for e in (-1, 1):
-                arrive(centre[SLICES - 1, -e], has_row[e])
+                arrive(centre[s, -e], has_row[e])
             for d in (-1, 1):
                 launch(corner[d], has_across & has_col[d])
+        for d in (-1, 1):
+            arrive(side[s, p, -d], has_col[d])
+            for e in (-1, 1):
+                launch(relay[s, p, d, e], relayed(s, e) & has_col[d])
 
     base_row, base_col = r * H - H, c * H - H
+    fetches["counts"].wait()
+    fetches["corners"].wait()
     local_row = [jnp.clip(corners[0, 0, q, 0] - base_row, 0, H) for q in range(CAP)]
     local_col = [jnp.clip(corners[0, 0, q, 1] - base_col, 0, H) for q in range(CAP)]
     lane = lax.broadcasted_iota(jnp.int32, (N, H), 1)
 
+    both_cols = has_col[-1] & has_col[1]
+
+    def bulk(amount, send_place, tag):
+        ref = {1: result.at[0], 2: result.at[pl.ds(0, 2)], 3: result, 6: ext0.at[pl.ds(0, 2)], 9: ext0}[amount]
+        return pltpu.make_async_remote_copy(
+            ref, ref, send_sem.at[send_place], recv_sem.at[tag], device_id=core_peer, device_id_type=MESH
+        )
+
     def wait_slice(s):
         fetches["obj", s].wait()
         for e in (-1, 1):
-            if s < SLICES - 1:
-                arrive(centre[s, -e], has_row[e])
-            for d in (-1, 1):
-                arrive(relay[s, d, -e], relayed(s, e) & has_col[d])
+            for sides in (1, 2):
+                amount = sides + (s < SLICES - 1)
+                ok = relayed(s, e) & (both_cols if sides == 2 else jnp.logical_not(both_cols))
+
+                @pl.when(ok)
+                def _():
+                    bulk(amount, 0, rows_tag[s, -e]).wait_recv()
+
         if s == SLICES - 1:
             for d in (-1, 1):
                 arrive(corner[-d], has_across & has_col[d])
@@ -263,16 +308,19 @@
         return [jnp.concatenate([jnp.concatenate(w, axis=0) for w in part_], axis=1) for part_ in (first, second)]
 
     def right_step(waves, one, two, before, after):
-        first, second = right_halves(waves, before)
-        first, second = right_product(first, one), right_product(second, two)
         result = []
-        for q in range(CAP):
-            rows = slice(q * N, (q + 1) * N)
-            pair = []
-            for p in range(2):
-                u, v = first[rows, p * H : (p + 1) * H], second[rows, p * H : (p + 1) * H]
-                pair.append(jnp.concatenate([u + v, u - v] if after else [u, v], axis=1))
-            result.append(tuple(pair))
+        for wave in waves:
+            blocks = []
+            for k in range(2):
+                rows = slice(k * H, (k + 1) * H)
+                first, second = right_halves([[v[rows] for v in wave]], before)
+                first, second = right_product(first, one), right_product(second, two)
+                pair = []
+                for p in range(2):
+                    u, v = first[:, p * H : (p + 1) * H], second[:, p * H : (p + 1) * H]
+                    pair.append(jnp.concatenate([u + v, u - v] if after else [u, v], axis=1))
+                blocks.append(pair)
+            result.append(tuple(jnp.concatenate([b[p] for b in blocks], axis=0) for p in range(2)))
         return result
 
     def left_step(waves, one, two, before, after):
@@ -323,15 +371,20 @@
     for s in range(SLICES):
         for d in (-1, 1):
             up_down[s, d] = make(
-                win[s].at[:, :, pl.ds(H * (1 + d), H), :], rz[s].at[(1 - d) // 2], (r + d, c), new_tag()
+                win[s].at[:, :, pl.ds(H * (1 + d), H), :], rz[s].at[(1 - d) // 2], (r + d, c), new_tag(),
+                ("strip", d) if s == 0 else ("row", d), has_row[d] & on_chip[d] if s == 0 else has_row[d], 3
             )
-            sides[s, d] = make(ts[s].at[(1 + d) // 2], ry[s].at[(1 - d) // 2], (r, c + d), new_tag())
+            sides[s, d] = make(ts[s].at[(1 + d) // 2], ry[s].at[(1 - d) // 2], (r, c + d), new_tag(), ("col", d), has_col[d], 1)
 
     corner_back = {
-        d: make(win[0].at[1 + d, :, across_rows, :], corner_in.at[(1 - d) // 2], (r, c + d), new_tag()) for d in (-1, 1)
+        d: make(
+            win[0].at[1 + d, :, across_rows, :], corner_in.at[(1 - d) // 2], (r, c + d), new_tag(),
+            ("corner", d), has_across & has_col[d], 1,
+        )
+        for d in (-1, 1)
     }
     far_row = (r + 2 * core - 1, c)
-    centre_back = make(corner_sum, rz[0].at[1 - core, 1], far_row, new_tag())
+    centre_back = make(corner_sum, rz[0].at[1 - core, 1], far_row, new_tag(), "across", has_across, 1)
 
     def place(s, back):
         for q in range(CAP):
@@ -350,6 +403,8 @@
                 for q in range(1, CAP):
                     total = total + pads[q, cb, p, pl.ds(H - local_row[q], 3 * H), :]
                 win[s][cb, p] = total
+
+    def send_rows(s):
         for d in (-1, 1):
             launch(up_down[s, d], has_row[d] & on_chip[d] if s == 0 else has_row[d])
         if s == 0:
@@ -366,23 +421,46 @@
         launch(centre_back, has_across)
 
     big, small = 4 * H, 4 * H // 64
-    step_a = make(part.at[pl.ds((1 - core) * big, big)], buf_a, core_peer, new_tag())
+    quarter = big // 4
+
+    def plane_rows(dz, base=0):
+        return pl.ds(base + (z + dz) % 4 * quarter, quarter)
+
+    step_a = {
+        dz: make(part.at[plane_rows(dz, (1 - core) * big)], buf_a.at[plane_rows(dz)], core_peer, new_tag(), "core", None, 0.5)
+        for dz in planes
+    }
     own_rows = pl.ds((z * 16 + c) * small, small)
-    out_tag, back_tag = new_tag(), new_tag()
-    step_b, step_c = [], []
+    out_tag = new_tag()
+    back_tags = {dz: new_tag() for dz in planes}
+    step_b, step_c = {}, {}
     for at, (dz, dx, dy) in enumerate(offsets):
         theirs = (z + dz) % 4 * 16 + (x + dx) % 4 * 4 + (y + dy) % 4
-        step_b.append(make(sum_a.at[pl.ds(theirs * small, small)], buf_b.at[at], device(dx, dy, dz), out_tag))
-        step_c.append(make(full_a.at[own_rows], full_a.at[own_rows], device(dx, dy, dz), back_tag))
-    all_b = make(buf_b, buf_b, core_peer, out_tag)
-    all_c = make(full_a.at[pl.ds(0, 63 * small)], full_a.at[pl.ds(0, 63 * small)], core_peer, back_tag)
-    step_d = make(full_a, full.at[pl.ds(core * big, big)], core_peer, new_tag())
+        step_b[dz, dx, dy] = make(sum_a.at[pl.ds(theirs * small, small)], buf_b.at[at], device(dx, dy, dz), out_tag, "out")
+        step_c[dz, dx, dy] = make(full_a.at[own_rows], full_a.at[own_rows], device(dx, dy, dz), back_tags[dz], "back")
+    all_b = make(buf_b, buf_b, core_peer, out_tag, "out")
+    all_c = {}
+    for dz in planes:
+        rows = pl.ds(0, (16 if dz else 15) * small)
+        all_c[dz] = make(full_a.at[rows], full_a.at[rows], core_peer, back_tags[dz], "back")
+    step_d = {
+        dz: make(full_a.at[plane_rows(4 - dz)], full.at[plane_rows(4 - dz)], core_peer, new_tag(), "core back", None, 0.5) for dz in planes
+    }
+
+    def store_probe(source, half, dz, sem):
+        at = (z + 4 - dz) % 4
+        return pltpu.make_async_copy(
+            source.at[plane_rows(4 - dz)],
+            probe_out.at[half, pl.ds(at % 2 * H, H), pl.ds(at // 2 * H, H)],
+            load_sem.at[sem],
+        )
 
     backs = {}
     for s in reversed(range(SLICES)):
         backs[s] = back
         if s == SLICES - 1:
             place(s, back)
+            send_rows(s)
         back = [times(get_patch(s, q), back[q]) for q in range(CAP)]
         if s > 0:
             back = prop(back)
@@ -391,7 +469,8 @@
     for p, value in enumerate((total_re, total_im)):
         for half in range(2):
             part[pl.ds((2 * p + half) * N, N), :] = value[:, half * H : (half + 1) * H]
-    launch(step_a)
+    for dz in planes:
+        launch(step_a[dz])
     pl.semaphore_wait(far_sem, 3)
 
     def rows_done(s):
@@ -420,59 +499,56 @@
         result[s] = total
         fetch(("out", s), result.at[s], out.at[s], 7 + s)
 
-    arrive(step_a)
-    sum_a[...] = part[pl.ds(core * big, big), :] + buf_a[...]
-    for copy in step_b:
-        copy.start()
+    for dz in planes:
+        arrive(step_a[dz])
+        sum_a[plane_rows(dz), :] = part[plane_rows(dz, core * big), :] + buf_a[plane_rows(dz), :]
+        for steps in offsets:
+            if steps[0] == dz:
+                step_b[steps].start()
     place(1, backs[1])
+    send_rows(1)
     place(0, backs[0])
+    send_rows(0)
     rows_done(2)
+    corners_done()
     all_b.wait_recv()
     total = sum_a[own_rows, :]
     for d in range(63):
         total = total + buf_b[d]
     full_a[own_rows, :] = total
-    for copy in step_c:
-        copy.start()
-    corners_done()
+    for steps in offsets:
+        step_c[steps].start()
     columns_done(2)
     rows_done(1)
     rows_done(0)
     columns_done(1)
-    all_c.wait_recv()
-    launch(step_d)
-    own_half = [pltpu.make_async_copy(probe_result.at[p], probe_out.at[p], load_sem.at[10]) for p in range(2)]
-    other_half = [pltpu.make_async_copy(probe_result.at[p], probe_out.at[p], load_sem.at[11]) for p in range(2)]
-    for p in range(2):
-        @pl.when(core == p)
-        def _():
-            for half in range(2):
-                probe_result[p, :, half * H : (half + 1) * H] = full_a[pl.ds(half * N, N), :]
-            own_half[p].start()
+    for dz in planes:
+        all_c[dz].wait_recv()
+        launch(step_d[dz])
+        store_probe(full_a, core, dz, 10 + dz).start()
     columns_done(0)
-    arrive(step_d)
-    for p in range(2):
-        @pl.when(core != p)
-        def _():
-            for half in range(2):
-                probe_result[p, :, half * H : (half + 1) * H] = full[pl.ds((2 * p + half) * N, N), :]
-            other_half[p].start()
-    own_half[0].wait()
-    other_half[0].wait()
+    for dz in planes:
+        arrive(step_d[dz])
+        store_probe(full, 1 - core, dz, 14 + dz).start()
+    for dz in planes:
+        store_probe(full_a, core, dz, 10 + dz).wait()
+        store_probe(full, 1 - core, dz, 14 + dz).wait()
     for s in range(SLICES):
         fetches["out", s].wait()
+    assert serial[0] == N_TAGS and len(groups) == N_GROUPS
     all_b.wait_send()
-    all_c.wait_send()
-    for copy, ok in sent:
-        if ok is None:
-            copy.wait_send()
-        else:
+    make(buf_b, buf_b, core_peer, out_tag, "back").wait_send()
+    for at, ok, amount in groups.values():
+        if amount and ok is None:
+            bulk(int(amount), at, 0).wait_send()
+        elif amount:
             @pl.when(ok)
             def _():
-                copy.wait_send()
-
-
-N_TAGS = SLICES * 8 + 2 + SLICES * 4 + 3 + 1 + 2 + 1
+                bulk(int(amount), at, 0).wait_send()
+
+
+N_TAGS = 48
+N_GROUPS = 21
 
 
 def finish(grad, probe_grad, out, probe_out, held, probe_held, sem):
@@ -491,14 +567,13 @@
 
 def on_device(object_tiles, probe_wave, slot_counts, slot_offsets, amplitudes):
     mats, orders = constant_matrices()
-    smem = pl.BlockSpec(memory_space=pltpu.SMEM)
     per_slice = lambda *shape: [pltpu.VMEM(shape, F32) for _ in range(SLICES)]
     shapes = (jax.ShapeDtypeStruct((SLICES, 2, H, H), F32), jax.ShapeDtypeStruct((2, N, N), F32))
     hbm = pl.BlockSpec(memory_space=pl.ANY)
     grads = pl.pallas_call(
         kernel,
         out_shape=shapes,
-        in_specs=[hbm, hbm, smem, smem, hbm, hbm, hbm],
+        in_specs=[hbm] * 7,
         out_specs=(hbm, hbm),
         scratch_shapes=[
             *per_slice(3, 2, 3 * H, H),
@@ -517,16 +592,17 @@
             pltpu.VMEM((4 * H, H), F32),
             pltpu.VMEM((63, 4 * H // 64, H), F32),
             pltpu.VMEM((4 * H, H), F32),
-            pltpu.VMEM((8 * H, H), F32),
+            pltpu.VMEM((4 * H, H), F32),
             pltpu.VMEM((2, N, N), F32),
             pltpu.VMEM((CAP, N, N), F32),
             pltpu.VMEM((10, 2, N, N), BF16),
             pltpu.VMEM((2, N, N), BF16),
             pltpu.VMEM((SLICES, 2, H, H), F32),
-            pltpu.VMEM((2, N, N), F32),
+            pltpu.SMEM((1, 1), jnp.int32),
+            pltpu.SMEM((1, 1, CAP, 2), jnp.int32),
+            pltpu.SemaphoreType.DMA((N_GROUPS,)),
             pltpu.SemaphoreType.DMA((N_TAGS,)),
-            pltpu.SemaphoreType.DMA((N_TAGS,)),
-            pltpu.SemaphoreType.DMA((12,)),
+            pltpu.SemaphoreType.DMA((20,)),
             pltpu.SemaphoreType.REGULAR,
             pltpu.SemaphoreType.REGULAR,
         ],

time: 53.6 us -> 51.6 us (0.963)
  the two profiles are of different devices: /device:TPU:34 before, /device:TPU:66 now
where the time goes in v4:
time: 51.6 us; the launch traced here: 51.5 us
  Pallas kernels  50.2 us (97%)
  between operations  1.28 us (2%)
    pallas_call x1, Pallas kernels, on_device(): pl.pallas_call(kernel, out_shape=shapes, in_specs=[hbm] * 7, out_specs=(h...  48.1 us
    pallas_call x1, Pallas kernels, on_device(): pl.pallas_call(finish, out_shape=shapes, in_specs=[hbm, hbm], out_specs=(...  2.02 us

profile of v4, /device:TPU:66, one launch (start us, length us, event | category | flops | bytes accessed | tf_op | source)
XLA Modules:
  0.0 51.5 jit_solution(6932633109397040698)
XLA Ops:
  1.3 48.1 %ptychography_step.1 = (f32[3,2,128,128]{3,2,1,0:T(8,128)}, f32[2,256,256]{2,1,0:T(8,128)}) custom-call(f32[3,2,128,128]{3,2,1,0:T(8,128)} %obj.1, f32[2,256,256]{2,1,0:T(8,128)} %probe_hbm.1, s32[1,1]{1,0:T(1,128)S(6)} %copy.9.counts_hbm, s32[1,1,2,2]{3,2,1,0:T(2,128)} %corners_hbm.1, f32[1,1,2,256,256]{4,3,2,1,0:T(8,128)} %amps_hbm.1, ...), custom_call_target="tpu_custom_call" | custom-call | tf_op jit(solution)/shard_map/ptychography_step/pallas_call | solution.py:573
  49.4 2.0 %results.1 = (f32[3,2,128,128]{3,2,1,0:T(8,128)}, f32[2,256,256]{2,1,0:T(8,128)}) custom-call(f32[3,2,128,128]{3,2,1,0:T(8,128)} %get-tuple-element.4.grad, f32[2,256,256]{2,1,0:T(8,128)} %get-tuple-element.5.probe_grad), custom_call_target="tpu_custom_call" | custom-call | tf_op jit(solution)/shard_map/results/pallas_call | solution.py:622

commit v5 on v4

--- a/solution.py
+++ b/solution.py
@@ -496,8 +496,7 @@
         total = result[s]
         for d in (-1, 1):
             total = total + jnp.where(has_col[d], ry[s][(1 + d) // 2], 0.0)
-        result[s] = total
-        fetch(("out", s), result.at[s], out.at[s], 7 + s)
+        out[s] = total
 
     for dz in planes:
         arrive(step_a[dz])
@@ -516,13 +515,13 @@
     for d in range(63):
         total = total + buf_b[d]
     full_a[own_rows, :] = total
-    for steps in offsets:
+    for steps in sorted(offsets, key=lambda v: (0, 1, 3, 2).index(v[0])):
         step_c[steps].start()
     columns_done(2)
     rows_done(1)
     rows_done(0)
     columns_done(1)
-    for dz in planes:
+    for dz in (0, 1, 3, 2):
         all_c[dz].wait_recv()
         launch(step_d[dz])
         store_probe(full_a, core, dz, 10 + dz).start()
@@ -533,8 +532,6 @@
     for dz in planes:
         store_probe(full_a, core, dz, 10 + dz).wait()
         store_probe(full, 1 - core, dz, 14 + dz).wait()
-    for s in range(SLICES):
-        fetches["out", s].wait()
     assert serial[0] == N_TAGS and len(groups) == N_GROUPS
     all_b.wait_send()
     make(buf_b, buf_b, core_peer, out_tag, "back").wait_send()
@@ -551,17 +548,12 @@
 N_GROUPS = 21
 
 
-def finish(grad, probe_grad, out, probe_out, held, probe_held, sem):
-    places = [(grad.at[s], held.at[s], out.at[s]) for s in range(SLICES)]
-    places += [(probe_grad.at[p], probe_held.at[p], probe_out.at[p]) for p in range(2)]
-    loads = [pltpu.make_async_copy(a, b, sem.at[0, i]) for i, (a, b, _) in enumerate(places)]
-    stores = [pltpu.make_async_copy(b, c, sem.at[1, i]) for i, (_, b, c) in enumerate(places)]
-    for copy in loads:
+def finish(grad, probe_grad, out, probe_out, sem):
+    copies = [pltpu.make_async_copy(grad.at[s], out.at[s], sem.at[s]) for s in range(SLICES)]
+    copies += [pltpu.make_async_copy(probe_grad.at[p], probe_out.at[p], sem.at[SLICES + p]) for p in range(2)]
+    for copy in copies:
         copy.start()
-    for load, store in zip(loads, stores):
-        load.wait()
-        store.start()
-    for copy in stores:
+    for copy in copies:
         copy.wait()
 
 
@@ -570,11 +562,13 @@
     per_slice = lambda *shape: [pltpu.VMEM(shape, F32) for _ in range(SLICES)]
     shapes = (jax.ShapeDtypeStruct((SLICES, 2, H, H), F32), jax.ShapeDtypeStruct((2, N, N), F32))
     hbm = pl.BlockSpec(memory_space=pl.ANY)
+    vmem = pl.BlockSpec(memory_space=pltpu.VMEM)
+    far_memory = lambda value: pltpu.with_memory_space_constraint(value, pltpu.HBM)
     grads = pl.pallas_call(
         kernel,
-        out_shape=shapes,
+        out_shape=tuple(pltpu.VMEM(shape.shape, F32) for shape in shapes),
         in_specs=[hbm] * 7,
-        out_specs=(hbm, hbm),
+        out_specs=(vmem, vmem),
         scratch_shapes=[
             *per_slice(3, 2, 3 * H, H),
             *per_slice(3, 2, 3 * H, H),
@@ -611,26 +605,22 @@
         ),
         name="ptychography_step",
     )(
-        object_tiles,
-        probe_wave,
+        far_memory(object_tiles),
+        far_memory(probe_wave),
         slot_counts,
-        slot_offsets,
-        amplitudes,
-        jnp.asarray(mats),
-        jnp.asarray(orders),
+        far_memory(slot_offsets),
+        far_memory(amplitudes),
+        far_memory(jnp.asarray(mats)),
+        far_memory(jnp.asarray(orders)),
     )
     return pl.pallas_call(
         finish,
         out_shape=shapes,
-        in_specs=[hbm, hbm],
+        in_specs=[vmem, vmem],
         out_specs=(hbm, hbm),
-        scratch_shapes=[
-            pltpu.VMEM((SLICES, 2, H, H), F32),
-            pltpu.VMEM((2, N, N), F32),
-            pltpu.SemaphoreType.DMA((2, SLICES + 2)),
-        ],
+        scratch_shapes=[pltpu.SemaphoreType.DMA((SLICES + 2,))],
         name="results",
-    )(*grads)
+    )(*(pltpu.with_memory_space_constraint(grad, pltpu.VMEM) for grad in grads))
 
 
 def solution(mesh):

time: 51.6 us -> 49.7 us (0.963)
  the two profiles are of different devices: /device:TPU:66 before, /device:TPU:1 now
where the time goes in v5:
time: 49.7 us; the launch traced here: 49.5 us
  Pallas kernels  48.2 us (97%)
  between operations  1.28 us (3%)
    pallas_call x1, Pallas kernels, on_device(): pl.pallas_call(kernel, out_shape=tuple((pltpu.VMEM(shape.shape, F32) for...  47.2 us

profile of v5, /device:TPU:1, one launch (start us, length us, event | category | flops | bytes accessed | tf_op | source)
XLA Modules:
  0.0 49.5 jit_solution(104863682464619816)
XLA Ops:
  1.3 47.2 %ptychography_step.1 = (f32[3,2,128,128]{3,2,1,0:T(8,128)S(1)}, f32[2,256,256]{2,1,0:T(8,128)S(1)}) custom-call(f32[3,2,128,128]{3,2,1,0:T(8,128)} %obj.1, f32[2,256,256]{2,1,0:T(8,128)} %probe_hbm.1, s32[1,1]{1,0:T(1,128)S(6)} %copy.9.counts_hbm, s32[1,1,2,2]{3,2,1,0:T(2,128)} %corners_hbm.1, f32[1,1,2,256,256]{4,3,2,1,0:T(8,128)} %amps_hbm.1, ...), custom_call_target="tpu_custom_call" | custom-call | tf_op jit(solution)/shard_map/ptychography_step/pallas_call | solution.py:567
  48.5 1.0 %results.1 = (f32[3,2,128,128]{3,2,1,0:T(8,128)}, f32[2,256,256]{2,1,0:T(8,128)}) custom-call(f32[3,2,128,128]{3,2,1,0:T(8,128)S(1)} %get-tuple-element.4.grad, f32[2,256,256]{2,1,0:T(8,128)S(1)} %get-tuple-element.5.probe_grad), custom_call_target="tpu_custom_call" | custom-call | tf_op jit(solution)/shard_map/results/pallas_call | solution.py:616

commit v6 on v5

--- a/solution.py
+++ b/solution.py
@@ -324,14 +324,13 @@
         return result
 
     def left_step(waves, one, two, before, after):
-        first, second = left_halves(waves, before)
-        first, second = left_product(one, first), left_product(two, second)
         result = []
-        for q in range(CAP):
-            cols = slice(q * N, (q + 1) * N)
+        for wave in waves:
+            first, second = left_halves([wave], before)
+            first, second = left_product(one, first), left_product(two, second)
             pair = []
             for p in range(2):
-                u, v = first[p * H : (p + 1) * H, cols], second[p * H : (p + 1) * H, cols]
+                u, v = first[p * H : (p + 1) * H], second[p * H : (p + 1) * H]
                 pair.append(jnp.concatenate([u + v, u - v] if after else [u, v], axis=0))
             result.append(tuple(pair))
         return result

time: 49.7 us -> 49.8 us (level); the launches traced: 49.5 us -> 48.8 us
  Pallas kernels: 48.2 us -> 47.5 us
    pallas_call x1, Pallas kernels: 47.2 us -> 46.6 us  [on_device(): pl.pallas_call(kernel, out_shape=tuple((pltpu.VMEM(shape.shape, F32) for...]
where the time goes in v6:
time: 49.8 us; the launch traced here: 48.8 us
  Pallas kernels  47.5 us (95%)
  between operations  1.28 us (3%)
    pallas_call x1, Pallas kernels, on_device(): pl.pallas_call(kernel, out_shape=tuple((pltpu.VMEM(shape.shape, F32) for...  46.6 us

profile of v6, /device:TPU:1, one launch (start us, length us, event | category | flops | bytes accessed | tf_op | source)
XLA Modules:
  0.0 48.8 jit_solution(15225170509119818016)
XLA Ops:
  1.3 46.6 %ptychography_step.1 = (f32[3,2,128,128]{3,2,1,0:T(8,128)S(1)}, f32[2,256,256]{2,1,0:T(8,128)S(1)}) custom-call(f32[3,2,128,128]{3,2,1,0:T(8,128)} %obj.1, f32[2,256,256]{2,1,0:T(8,128)} %probe_hbm.1, s32[1,1]{1,0:T(1,128)S(6)} %copy.9.counts_hbm, s32[1,1,2,2]{3,2,1,0:T(2,128)} %corners_hbm.1, f32[1,1,2,256,256]{4,3,2,1,0:T(8,128)} %amps_hbm.1, ...), custom_call_target="tpu_custom_call" | custom-call | tf_op jit(solution)/shard_map/ptychography_step/pallas_call | solution.py:566
  47.8 1.0 %results.1 = (f32[3,2,128,128]{3,2,1,0:T(8,128)}, f32[2,256,256]{2,1,0:T(8,128)}) custom-call(f32[3,2,128,128]{3,2,1,0:T(8,128)S(1)} %get-tuple-element.4.grad, f32[2,256,256]{2,1,0:T(8,128)S(1)} %get-tuple-element.5.probe_grad), custom_call_target="tpu_custom_call" | custom-call | tf_op jit(solution)/shard_map/results/pallas_call | solution.py:615

commit v7 on v6

--- a/solution.py
+++ b/solution.py
@@ -548,8 +548,12 @@
 
 
 def finish(grad, probe_grad, out, probe_out, sem):
-    copies = [pltpu.make_async_copy(grad.at[s], out.at[s], sem.at[s]) for s in range(SLICES)]
-    copies += [pltpu.make_async_copy(probe_grad.at[p], probe_out.at[p], sem.at[SLICES + p]) for p in range(2)]
+    places = [(grad.at[s, p], out.at[s, p]) for s in range(SLICES) for p in range(2)]
+    for p in range(2):
+        for k in range(4):
+            rows = pl.ds(k * N // 4, N // 4)
+            places.append((probe_grad.at[p, rows], probe_out.at[p, rows]))
+    copies = [pltpu.make_async_copy(a, b, sem.at[i]) for i, (a, b) in enumerate(places)]
     for copy in copies:
         copy.start()
     for copy in copies:
@@ -617,7 +621,7 @@
         out_shape=shapes,
         in_specs=[vmem, vmem],
         out_specs=(hbm, hbm),
-        scratch_shapes=[pltpu.SemaphoreType.DMA((SLICES + 2,))],
+        scratch_shapes=[pltpu.SemaphoreType.DMA((2 * SLICES + 8,))],
         name="results",
     )(*(pltpu.with_memory_space_constraint(grad, pltpu.VMEM) for grad in grads))
 

time: 49.8 us -> 49.8 us (level)
  no operation moved by 1% of the time
where the time goes in v7:
time: 49.8 us; the launch traced here: 48.9 us
  Pallas kernels  47.6 us (96%)
  between operations  1.28 us (3%)
    pallas_call x1, Pallas kernels, on_device(): pl.pallas_call(kernel, out_shape=tuple((pltpu.VMEM(shape.shape, F32) for...  46.6 us
    pallas_call x1, Pallas kernels, on_device(): pl.pallas_call(finish, out_shape=shapes, in_specs=[vmem, vmem], out_specs...  1.03 us

profile of v7, /device:TPU:1, one launch (start us, length us, event | category | flops | bytes accessed | tf_op | source)
XLA Modules:
  0.0 48.9 jit_solution(1080504436495683081)
XLA Ops:
  1.3 46.6 %ptychography_step.1 = (f32[3,2,128,128]{3,2,1,0:T(8,128)S(1)}, f32[2,256,256]{2,1,0:T(8,128)S(1)}) custom-call(f32[3,2,128,128]{3,2,1,0:T(8,128)} %obj.1, f32[2,256,256]{2,1,0:T(8,128)} %probe_hbm.1, s32[1,1]{1,0:T(1,128)S(6)} %copy.9.counts_hbm, s32[1,1,2,2]{3,2,1,0:T(2,128)} %corners_hbm.1, f32[1,1,2,256,256]{4,3,2,1,0:T(8,128)} %amps_hbm.1, ...), custom_call_target="tpu_custom_call" | custom-call | tf_op jit(solution)/shard_map/ptychography_step/pallas_call | solution.py:570
  47.8 1.0 %results.1 = (f32[3,2,128,128]{3,2,1,0:T(8,128)}, f32[2,256,256]{2,1,0:T(8,128)}) custom-call(f32[3,2,128,128]{3,2,1,0:T(8,128)S(1)} %get-tuple-element.4.grad, f32[2,256,256]{2,1,0:T(8,128)S(1)} %get-tuple-element.5.probe_grad), custom_call_target="tpu_custom_call" | custom-call | tf_op jit(solution)/shard_map/results/pallas_call | solution.py:619
